TPU v7x, 256 devices: a whole 4x4x8 slice. The times are simulated.
256 devices in a mesh: row: 16 (over z_hi, y), col: 16 (over z_lo, x, core).
Axes of the slice: x: 4, y: 4, z: 8 (z_hi: 4, z_lo: 2; z = z_hi * 2 + z_lo), core: 2. Of those that a mesh axis runs over, the one named last changes fastest.
Arguments:
- out_grad: bfloat16 [65536, 128], P(('row', 'col')), may hold values from -6 to 6
- preact: bfloat16 [65536, 128], P(('row', 'col')), may hold values from -6 to 6
- aggregated: bfloat16 [65536, 128], P(('row', 'col')), may hold values from -6 to 6
- weight: bfloat16 [128, 128], replicated, may hold values from -0.5 to 0.5
- tiles: bfloat16 [16, 16, 256, 128, 128], P('row', 'col'), may hold values from -0.09375 to 0.09375
- tile_coords: int32 [16, 16, 2, 256], P('row', 'col'), may hold values from 0 to 31, as said below
- tile_count: int32 [16, 16], P('row', 'col'), may hold values from 32 to 256, as said below
Outputs:
- input_grad: bfloat16 [65536, 128], P(('row', 'col'))
- weight_grad: float32 [128, 128], replicated
Inputs may be any that keep to these rules, and one draw needn't show every extreme that they name: `tile_coords`: on each device the first tile_count slots hold distinct tiles, in non-decreasing row block; row blocks are below 32 and column blocks below 32; entries of later slots are not used. `tile_count`: some device uses all 256 slots.
All inputs are finite; a program needn't handle non-finite values.
Results may differ from a plain program's by a relative error of at most 0.0049.
Values may be sent and summed in bfloat16 or wider, within the bound.
No kernel may reach another device: no remote copies, remote signals or barrier semaphores. Data moves between devices by JAX's collectives and lax.ppermute only.
A program may use at most 64 MiB of HBM per device.

v0:
```python
import math

import jax
import jax.numpy as jnp
from jax import lax
from jax.sharding import PartitionSpec as P

group_tiles = 16


def tile_pass(
    running_sum, tile_vals, row_pos, col_pos, order, lowest, highest, source, src_start, dst_start
):
    tile_size = tile_vals.shape[1]
    src_len = source.shape[0]
    dst_len = running_sum.shape[0] - 2 * tile_size
    padded = jnp.pad(source, ((tile_size, tile_size), (0, 0)))
    slot_count = tile_vals.shape[0]
    group_count = (highest - lowest + group_tiles - 1) // group_tiles

    def one_group(group_step, carried):
        positions = lowest + group_step * group_tiles + jnp.arange(group_tiles, dtype=jnp.int32)
        usable = positions < highest
        positions = jnp.minimum(positions, slot_count - 1)
        slot_ids = jnp.take(order, positions)
        chosen = jnp.take(tile_vals, slot_ids, axis=0)
        src_offset = jnp.take(row_pos, slot_ids) * tile_size - src_start + tile_size
        dst_offset = jnp.take(col_pos, slot_ids) * tile_size - dst_start + tile_size
        in_range = usable & (src_offset > 0) & (src_offset < src_len + tile_size)
        in_range = in_range & (dst_offset > 0) & (dst_offset < dst_len + tile_size)
        src_offset = jnp.clip(src_offset, 0, src_len + tile_size)
        dst_offset = jnp.clip(dst_offset, 0, dst_len + tile_size)
        src_rows = jax.vmap(lambda offset: lax.dynamic_slice_in_dim(padded, offset, tile_size, 0))(
            src_offset
        )
        src_rows = jnp.where(in_range[:, None, None], src_rows, jnp.zeros_like(src_rows))
        products = jnp.einsum("tab,taf->tbf", chosen, src_rows, preferred_element_type=jnp.float32)
        for member in range(group_tiles):
            current = lax.dynamic_slice_in_dim(carried, dst_offset[member], tile_size, 0)
            carried = lax.dynamic_update_slice_in_dim(
                carried, current + products[member], dst_offset[member], 0
            )
        return carried

    return lax.fori_loop(0, group_count, one_group, running_sum)


def body(out_grad, preact, aggregated, weight, tiles, tile_coords, tile_count):
    tile_size = tiles.shape[-1]
    tile_vals = tiles.reshape(tiles.shape[2], tile_size, tile_size)
    row_pos = tile_coords[0, 0, 0]
    col_pos = tile_coords[0, 0, 1]
    in_use = tile_count[0, 0]
    grad_pre = jnp.where(preact > 0, out_grad, jnp.zeros_like(out_grad))
    local_weight = lax.dot_general(
        aggregated, grad_pre, (((0,), (0,)), ((), ())), preferred_element_type=jnp.float32
    )
    node_rows = out_grad.shape[0]
    weight_scale = 1.0 / math.sqrt(node_rows * lax.axis_size("row") * lax.axis_size("col"))
    weight_grad = lax.psum(local_weight, ("row", "col")) * weight_scale
    grad_agg = lax.dot_general(
        grad_pre, weight, (((1,), (1,)), ((), ())), preferred_element_type=jnp.float32
    ).astype(jnp.bfloat16)
    col_rows = node_rows * lax.axis_size("row")
    features = weight.shape[0]
    empty_sum = jnp.zeros((col_rows + 2 * tile_size, features), jnp.float32)
    slot_count = tile_vals.shape[0]
    slot_ids = jnp.arange(slot_count, dtype=jnp.int32)
    gathered = lax.all_gather(grad_agg, "col", axis=0, tiled=True)
    partial_value = tile_pass(
        empty_sum, tile_vals, row_pos, col_pos, slot_ids, 0, in_use, gathered, 0, 0
    )
    summed = lax.psum_scatter(
        partial_value[tile_size : tile_size + col_rows], "row", scatter_dimension=0, tiled=True
    )
    return (summed.astype(jnp.bfloat16), weight_grad)


def solution(mesh):
    return jax.shard_map(
        body,
        mesh=mesh,
        in_specs=(
            P(("row", "col"), None),
            P(("row", "col"), None),
            P(("row", "col"), None),
            P(),
            P("row", "col", None, None, None),
            P("row", "col", None, None),
            P("row", "col"),
        ),
        out_specs=(P(("row", "col"), None), P()),
        check_vma=False,
    )
```

profile of v0, /device:TPU:2, one launch (start us, length us, event | category | flops | bytes accessed | tf_op | source)
XLA Modules:
  0.0 1751.2 jit_solution(10815119858041975286)
XLA Ops:
  8.1 1.7 convolution_convert_fusion
  9.8 1.7 convolution_bitcast_fusion
  13.0 36.0 %all-gather.2.cloned.1.call-done = bf16[4096,128]{1,0:T(8,128)(2,1)} async-done(((bf16[256,128]{1,0:T(8,128)(2,1)}), bf16[4096,128]{1,0:T(8,128)(2,1)}) %all-gather.2.cloned.1.call-update) | async-done | bytes 1048592 | tf_op jit(solution)/shard_map/all_gather | solution.py:69
  51.9 200.1 %while.18 = (s32[]{:T(128)}, f32[4352,128]{1,0:T(8,128)}, s32[]{:T(128)}, s32[256]{0:T(256)S(1)}, bf16[256,128,128]{2,1,0:T(8,128)(2,1)}, /*index=5*/s32[]{:T(12...) while((s32[]{:T(128)}, f32[4352,128]{1,0:T(8,128)}, ...), condition=%wide.region_1.3_spmd.clone.clone, body=%wide.region_0.0_spmd.clone.sunk.clone | while | flops 67898192 | bytes 12660522 | solution.py:45
  57.3 22.4 %while.17 = (s32[]{:T(128)}, bf16[4352,128]{1,0:T(8,128)(2,1)S(1)}, s32[16,2]{0,1:T(2,128)S(1)}, bf16[16,128,128]{2,1,0:T(8,128)(2,1)S(1)}, s32[]{:T(128)}) while((s32[]{:T(128)}, bf16[4352,128]{1,0:T(8,128)(2,1)S(1)}, s32[16,2]{0,1:T(2,128)S(1)}, bf16[16,128,128]{2,1,0:T(8,128)(2,1)S(1)}, s32[]{:T(128)}) %tuple.75), condition=%wide.while_cond, body=%wide.while_body.sunk | while | flops 2 | bytes 65633 | solution.py:33
  79.7 4.0 gather_fusion.3
  89.5 1.5 dynamic_update_slice.97
  98.5 1.5 dynamic_update_slice.99
  102.6 1.5 dynamic_update_slice.100
  111.4 1.5 dynamic_update_slice.102
  115.8 1.5 dynamic_update_slice.103
  124.5 1.5 dynamic_update_slice.105
  137.0 1.5 dynamic_update_slice.108
  141.4 1.5 dynamic_update_slice.109
  145.8 1.5 dynamic_update_slice.110
  150.3 1.5 dynamic_update_slice.111
  157.3 22.4 %while.17 = (s32[]{:T(128)}, bf16[4352,128]{1,0:T(8,128)(2,1)S(1)}, s32[16,2]{0,1:T(2,128)S(1)}, bf16[16,128,128]{2,1,0:T(8,128)(2,1)S(1)}, s32[]{:T(128)}) while((s32[]{:T(128)}, bf16[4352,128]{1,0:T(8,128)(2,1)S(1)}, s32[16,2]{0,1:T(2,128)S(1)}, bf16[16,128,128]{2,1,0:T(8,128)(2,1)S(1)}, s32[]{:T(128)}) %tuple.75), condition=%wide.while_cond, body=%wide.while_body.sunk | while | flops 2 | bytes 65633 | solution.py:33
  179.7 4.0 gather_fusion.3
  185.2 1.5 dynamic_update_slice.96
  189.5 1.5 dynamic_update_slice.97
  193.9 1.5 dynamic_update_slice.98
  202.7 1.6 dynamic_update_slice.100
  207.2 1.5 dynamic_update_slice.101
  211.4 1.6 dynamic_update_slice.102
  220.2 1.5 dynamic_update_slice.104
  224.6 1.5 dynamic_update_slice.105
  228.7 1.5 dynamic_update_slice.106
  245.8 1.5 dynamic_update_slice.110
  250.4 1.5 dynamic_update_slice.111
  251.9 3.0 slice.123
  255.0 2.2 all-reduce.4.cloned.1.call-done
  258.8 1483.4 %reduce-scatter.2.cloned.1.call-done = f32[256,128]{1,0:T(8,128)} async-done(((f32[4096,128]{1,0:T(8,128)}), f32[256,128]{1,0:T(8,128)}) %reduce-scatter.2.cloned.1.call-update) | async-done | bytes 131088 | tf_op jit(solution)/shard_map/reduce_scatter | solution.py:73
  (185 shorter events, 105.9 us)
Async XLA Ops:
  8.0 1.8 copy-start
  8.0 41.0 %all-gather.2.cloned.1.call-start = ((), (), s32[]{:S(2)}) async-start(), calls=%async_computation.1 | async-start | bytes 1114112 | tf_op jit(solution)/shard_map/all_gather | solution.py:69
  9.8 247.4 %all-reduce.4.cloned.1.call-start = ((), (), s32[]{:S(2)}) async-start(), calls=%async_computation.3 | async-start | bytes 131072 | tf_op jit(solution)/shard_map/psum | solution.py:60
  11.5 1730.6 %reduce-scatter.2.cloned.1.call-start = ((), (), s32[]{:S(2)}) async-start(), calls=%async_computation.2 | async-start | bytes 2228224 | tf_op jit(solution)/shard_map/reduce_scatter | solution.py:73
  84.1 4.4 copy-start.1
  184.2 4.4 copy-start.1
Sparse Core Ops, SparseCore 0:
  11.3 37.6 all-gather.1
  255.1 1487.0 reduce-scatter.1
Sparse Core Ops, SparseCore 1:
  17.2 239.9 all-reduce.3
where the time goes:
time: 1790 us; the launch traced here: 1750 us
  waiting for transfers between devices  1520 us (85%)
  local copies, waits for them, and re-layouts  114 us (6%)
  loops' own time  60.5 us (3%)
  other arithmetic  34 us (2%)
    reduce_scatter x1, waiting for transfers between devices, body(): lax.psum_scatter(partial_value[tile_size:tile_size + col_rows], 'row', sc...  1480 us
    another operation x1, loops' own time, tile_pass(): return lax.fori_loop(0, group_count, one_group, running_sum)  59.9 us
    dynamic_update_slice x32, local copies, waits for them, and re-layouts, one_group(): lax.dynamic_update_slice_in_dim(carried, current + products[member], dst_...  49.5 us
    gather x96, local copies, waits for them, and re-layouts  44.1 us
    all_gather x1, waiting for transfers between devices, body(): gathered = lax.all_gather(grad_agg, 'col', axis=0, tiled=True)  36 us
  transfers between devices with their start and end apart: 3, of which 3 were waited for; matrix products, arithmetic and copies ran while one was open for 9% of the time, Pallas kernels for 0%

commit v1 on v0

v1 whole, which is shorter than its diff:
```python
import functools
import itertools

import jax
import jax.numpy as jnp
from jax import lax
from jax.experimental import pallas as pl
from jax.experimental.pallas import tpu as pltpu
from jax.sharding import Mesh, PartitionSpec as P

bf16 = jnp.bfloat16
f32 = jnp.float32
T = 128
ROWS = ("zh", "y")
COLS = ("zl", "x", "core")
GROUP = 16
UNROLL = 8
LIMIT = 48 * 1024 * 1024

PEERS = [(dz, dx) for dz in range(2) for dx in range(4)]


def spec(space=pltpu.VMEM):
    return pl.BlockSpec(memory_space=space)


def split_parts(value):
    high = value.astype(bf16)
    low = (value - high.astype(f32)).astype(bf16)
    return high, low


def join_parts(high, low):
    return high.astype(f32) + low.astype(f32)


def ring_sum(own, received):
    return (own + received[1]) + (received[0] + received[2])


def prep_kernel(pos, og, pre, agg, weight, *refs):
    messages, wbuf = refs[:8], refs[8]
    zl, x = pos[2], pos[3]
    grad_pre = jnp.where(pre[...] > 0, og[...], jnp.zeros_like(og))
    g_t = lax.dot_general(
        weight[...], grad_pre, (((1,), (1,)), ((), ())), preferred_element_type=f32
    ).astype(bf16)
    wbuf[...] = lax.dot_general(
        agg[...], grad_pre, (((0,), (0,)), ((), ())), preferred_element_type=f32
    )
    for (dz, dx), message in zip(PEERS, messages):
        target = ((zl + dz) % 2) * 4 + (x + dx) % 4
        high, low = split_parts(wbuf[pl.ds(pl.multiple_of(target * 16, 16), 16), :])
        message[0:T, :] = g_t
        message[T : T + 16, 0:T] = high
        message[T : T + 16, T : 2 * T] = low


def tile_kernel(pos, count_ref, coords, *refs):
    own, other = refs[0:8], refs[8:16]
    tiles = refs[16]
    keep, keep_w, sends = refs[17], refs[18], refs[19:22]
    tile_buf, grads, acc, sems = refs[22:]
    y, zl, x, core = pos[1], pos[2], pos[3], pos[4]
    count = count_ref[0]
    slots = tiles.shape[0]

    def fetch(group):
        part = pl.ds(group * GROUP, GROUP)
        return pltpu.make_async_copy(tiles.at[part], tile_buf.at[part], sems.at[group])

    for group in range(slots // GROUP):

        @pl.when(group * GROUP < count)
        def _():
            fetch(group).start()

    sums = [jnp.zeros((16, T), f32)] * 2
    for i, (dz, dx) in enumerate(PEERS):
        shard = ((zl + 2 - dz) % 2) * 4 + (x + 4 - dx) % 4
        for side, (message, at) in enumerate(((own[i], core), (other[i], 1 - core))):
            base = (shard * 2 + at) * 2
            grads[base] = message[0:T, 0:T]
            grads[base + 1] = message[0:T, T : 2 * T]
            sums[side] += join_parts(message[T : T + 16, 0:T], message[T : T + 16, T : 2 * T])

    acc[...] = jnp.zeros_like(acc)
    dump = acc.shape[0] - 1

    @pl.loop(0, (count + GROUP - 1) // GROUP)
    def _(group):
        fetch(group).wait()

        @pl.loop(0, GROUP // UNROLL)
        def _(part):
            for u in range(UNROLL):
                k = group * GROUP + part * UNROLL + u
                live = k < count
                p = jnp.where(live, coords[0, k], 0)
                q = jnp.where(live, coords[1, k], dump)
                acc[q] += jnp.dot(grads[p], tile_buf[k], preferred_element_type=f32)

    high, low = split_parts(sums[0] + sums[1])
    for d in range(4):
        for zh in range(4):
            for h in range(2):
                q = (zh * 4 + (y + d) % 4) * 2 + h
                rows = pl.ds((zh * 2 + h) * T, T)
                if d == 0:
                    keep[rows, :] = acc[q]
                else:
                    sends[d - 1][rows, :] = acc[q].astype(bf16)
        if d:
            sends[d - 1][1024:1040, :] = high
            sends[d - 1][1040:1056, :] = low
    keep_w[...] = join_parts(high, low)


def y_kernel(pos, keep, keep_w, r1, r2, r3, keep_z, keep_zw, s1, s2, s3):
    zh_me = pos[0]
    parts = [join_parts(r[1024:1040, :], r[1040:1056, :]) for r in (r1, r2, r3)]
    high, low = split_parts(ring_sum(keep_w[...], parts))
    keep_zw[...] = join_parts(high, low)
    for d, out in enumerate((keep_z, s1, s2, s3)):
        rows = pl.ds(pl.multiple_of(((zh_me + d) % 4) * 256, 256), 256)
        total = keep[rows, :]
        for r in (r1, r2, r3):
            total += r[rows, :].astype(f32)
        if d == 0:
            out[...] = total
        else:
            out[0:256, :] = total.astype(bf16)
            out[256:272, :] = high
            out[272:288, :] = low


def z_kernel(keep_z, keep_zw, r1, r2, r3, out, chunk_out):
    parts = [join_parts(r[256:272, :], r[272:288, :]) for r in (r1, r2, r3)]
    chunk_out[...] = ring_sum(keep_zw[...], parts)
    for h in range(2):
        rows = pl.ds(h * T, T)
        total = keep_z[rows, :]
        for r in (r1, r2, r3):
            total += r[rows, :].astype(f32)
        out[rows, :] = total.T.astype(bf16)


def weight_kernel(scale, pos, *refs):
    chunks, out = refs[:8], refs[8]
    zl, x = pos[2], pos[3]
    for (dz, dx), chunk in zip(PEERS, chunks):
        shard = ((zl + 2 - dz) % 2) * 4 + (x + 4 - dx) % 4
        out[pl.ds(pl.multiple_of(shard * 16, 16), 16), :] = chunk[...] * scale


def call(kernel, out_shape, in_specs, scratch=(), cost=None):
    return pl.pallas_call(
        kernel,
        out_shape=out_shape,
        in_specs=in_specs,
        out_specs=jax.tree.map(lambda _: spec(), out_shape),
        scratch_shapes=list(scratch),
        compiler_params=pltpu.CompilerParams(vmem_limit_bytes=LIMIT),
        cost_estimate=cost,
    )


def struct(*shape, dtype=bf16):
    return jax.ShapeDtypeStruct(shape, dtype)


def peer_perm(dz, dx):
    pairs = itertools.product(range(2), range(4))
    return [(z * 4 + x, ((z + dz) % 2) * 4 + (x + dx) % 4) for z, x in pairs]


def body(out_grad, preact, aggregated, weight, tiles, tile_coords, tile_count):
    smem, vmem = spec(pltpu.SMEM), spec()
    pos = jnp.stack([lax.axis_index(a) for a in ROWS + COLS]).astype(jnp.int32)
    messages = call(
        prep_kernel,
        [struct(T + 16, 2 * T)] * 8,
        [smem] + [vmem] * 4,
        [pltpu.VMEM((T, T), f32)],
    )(pos, out_grad, preact, aggregated, weight)
    own = [messages[0]]
    for (dz, dx), message in list(zip(PEERS, messages))[1:]:
        own.append(lax.ppermute(message, ("zl", "x"), peer_perm(dz, dx)))
    other = [lax.ppermute(m, "core", [(0, 1), (1, 0)]) for m in own]

    slots = tiles.shape[2]
    keep, keep_w, *sends = call(
        tile_kernel,
        [struct(1024, T, dtype=f32), struct(16, T, dtype=f32)] + [struct(1056, T)] * 3,
        [smem] * 3 + [vmem] * 16 + [spec(pl.ANY)],
        [
            pltpu.VMEM((slots, T, T), bf16),
            pltpu.VMEM((32, T, T), bf16),
            pltpu.VMEM((33, T, T), f32),
            pltpu.SemaphoreType.DMA((slots // GROUP,)),
        ],
        pl.CostEstimate(flops=slots * 2 * T**3, bytes_accessed=slots * T * T * 2, transcendentals=0),
    )(
        pos,
        tile_count.reshape(1),
        tile_coords.reshape(2, slots),
        *own,
        *other,
        tiles.reshape(slots, T, T),
    )
    turn = lambda d: [(i, (i + d) % 4) for i in range(4)]
    got = [lax.ppermute(s, "y", turn(d)) for d, s in zip((1, 2, 3), sends)]
    keep_z, keep_zw, *sends = call(
        y_kernel,
        [struct(256, T, dtype=f32), struct(16, T, dtype=f32)] + [struct(288, T)] * 3,
        [smem] + [vmem] * 5,
    )(pos, keep, keep_w, *got)
    got = [lax.ppermute(s, "zh", turn(d)) for d, s in zip((1, 2, 3), sends)]
    input_grad, chunk = call(
        z_kernel, [struct(256, T), struct(16, T, dtype=f32)], [vmem] * 5
    )(keep_z, keep_zw, *got)
    chunks = [chunk]
    for dz, dx in PEERS[1:]:
        chunks.append(lax.ppermute(chunk, ("zl", "x"), peer_perm(dz, dx)))
    devices = 1
    for a in ROWS + COLS:
        devices *= lax.axis_size(a)
    scale = 1.0 / (out_grad.shape[0] * devices) ** 0.5
    weight_grad = call(
        functools.partial(weight_kernel, scale),
        struct(T, T, dtype=f32),
        [smem] + [vmem] * 8,
    )(pos, *chunks)
    return input_grad, weight_grad


def solution(mesh):
    fine = Mesh(mesh.devices.reshape(4, 4, 2, 4, 2), ROWS + COLS)
    every = ROWS + COLS
    return jax.shard_map(
        body,
        mesh=fine,
        in_specs=(
            P(every, None),
            P(every, None),
            P(every, None),
            P(),
            P(ROWS, COLS, None, None, None),
            P(ROWS, COLS, None, None),
            P(ROWS, COLS),
        ),
        out_specs=(P(every, None), P()),
        check_vma=False,
    )
```

time: 1790 us -> 78.2 us (0.04)
  the two profiles are of different devices: /device:TPU:2 before, /device:TPU:24 now
where the time goes in v1:
time: 78.2 us; the launch traced here: 77.5 us
  starting transfers between devices  42.2 us (54%)
  waiting for transfers between devices  23.7 us (30%)
  Pallas kernels  6.18 us (8%)
  local copies, waits for them, and re-layouts  4.04 us (5%)
  between operations  1.37 us (2%)
    ppermute x7, starting transfers between devices, body(): own.append(lax.ppermute(message, ('zl', 'x'), peer_perm(dz, dx)))  11.9 us
    ppermute x3, waiting for transfers between devices, body(): got = [lax.ppermute(s, 'y', turn(d)) for d, s in zip((1, 2, 3), sends)]  11.8 us
    ppermute x7, starting transfers between devices, body(): chunks.append(lax.ppermute(chunk, ('zl', 'x'), peer_perm(dz, dx)))  11.5 us
    ppermute x3, starting transfers between devices, body(): got = [lax.ppermute(s, 'zh', turn(d)) for d, s in zip((1, 2, 3), sends)]  10.6 us
    ppermute x3, starting transfers between devices, body(): got = [lax.ppermute(s, 'y', turn(d)) for d, s in zip((1, 2, 3), sends)]  6.46 us
    ppermute x3, waiting for transfers between devices, body(): got = [lax.ppermute(s, 'zh', turn(d)) for d, s in zip((1, 2, 3), sends)]  4.52 us
    ppermute x7, waiting for transfers between devices, body(): chunks.append(lax.ppermute(chunk, ('zl', 'x'), peer_perm(dz, dx)))  4.3 us
    unnamed x10, local copies, waits for them, and re-layouts  3.96 us
  transfers between devices with their start and end apart: 28, of which 12 were waited for; matrix products, arithmetic and copies ran while one was open for 0% of the time, Pallas kernels for 0%

profile of v1, /device:TPU:24, one launch (start us, length us, event | category | flops | bytes accessed | tf_op | source)
XLA Modules:
  0.0 77.5 jit_solution(6058378756445036519)
XLA Ops:
  0.7 0.8 %copy-done = bf16[256,128]{1,0:T(8,128)(2,1)S(1)} copy-done((bf16[256,128]{1,0:T(8,128)(2,1)S(1)}, bf16[256,128]{1,0:T(8,128)(2,1)}, u32[]{:S(2)}) %copy-start) | copy-done | bytes 65560
  1.6 0.8 %copy-done.1 = bf16[256,128]{1,0:T(8,128)(2,1)S(1)} copy-done((bf16[256,128]{1,0:T(8,128)(2,1)S(1)}, bf16[256,128]{1,0:T(8,128)(2,1)}, u32[]{:S(2)}) %copy-start.1) | copy-done | bytes 65560
  2.4 0.8 %copy-done.2 = bf16[256,128]{1,0:T(8,128)(2,1)S(1)} copy-done((bf16[256,128]{1,0:T(8,128)(2,1)S(1)}, bf16[256,128]{1,0:T(8,128)(2,1)}, u32[]{:S(2)}) %copy-start.2) | copy-done | bytes 65560
  3.2 0.8 copy-done.3
  4.0 0.8 shard_map.86
  4.8 1.6 %collective-permute-start = (bf16[144,256]{1,0:T(8,128)(2,1)S(1)}, bf16[144,256]{1,0:T(8,128)(2,1)S(1)}, u32[]{:S(2)}, u32[]{:S(2)}) collective-permute-start(bf16[144,256]{1,0:T(8,128)(2,1)S(1)} %get-tuple-element.23), channel_id=1, source_target_pairs={{0,2},{2,4},{4,6},{6,0},{8,10},{10,12},{12,14},{14,8},{1,3},{3,5},... | collective-permute-start | bytes 221192 | tf_op jit(solution)/shard_map/ppermute | solution.py:188
  6.3 2.7 %collective-permute-start.1 = (bf16[144,256]{1,0:T(8,128)(2,1)S(1)}, bf16[144,256]{1,0:T(8,128)(2,1)S(1)}, u32[]{:S(2)}, u32[]{:S(2)}) collective-permute-start(bf16[144,256]{1,0:T(8,128)(2,1)S(1)} %get-tuple-element.24), channel_id=1, source_target_pairs={{0,4},{2,6},{4,0},{6,2},{8,12},{10,14},{12,8},{14,10},{1,5},{3,7},... | collective-permute-start | bytes 221192 | tf_op jit(solution)/shard_map/ppermute | solution.py:188
  9.1 1.4 %collective-permute-start.2 = (bf16[144,256]{1,0:T(8,128)(2,1)S(1)}, bf16[144,256]{1,0:T(8,128)(2,1)S(1)}, u32[]{:S(2)}, u32[]{:S(2)}) collective-permute-start(bf16[144,256]{1,0:T(8,128)(2,1)S(1)} %get-tuple-element.25), channel_id=1, source_target_pairs={{0,6},{2,0},{4,2},{6,4},{8,14},{10,8},{12,10},{14,12},{1,7},{3,1},... | collective-permute-start | bytes 221192 | tf_op jit(solution)/shard_map/ppermute | solution.py:188
  10.5 1.9 %collective-permute-start.3 = (bf16[144,256]{1,0:T(8,128)(2,1)S(1)}, bf16[144,256]{1,0:T(8,128)(2,1)S(1)}, u32[]{:S(2)}, u32[]{:S(2)}) collective-permute-start(bf16[144,256]{1,0:T(8,128)(2,1)S(1)} %get-tuple-element.26), channel_id=1, source_target_pairs={{0,8},{2,10},{4,12},{6,14},{8,0},{10,2},{12,4},{14,6},{1,9},{3,11}... | collective-permute-start | bytes 221192 | tf_op jit(solution)/shard_map/ppermute | solution.py:188
  12.6 2.2 %collective-permute-start.5 = (bf16[144,256]{1,0:T(8,128)(2,1)S(1)}, bf16[144,256]{1,0:T(8,128)(2,1)S(1)}, u32[]{:S(2)}, u32[]{:S(2)}) collective-permute-start(bf16[144,256]{1,0:T(8,128)(2,1)S(1)} %get-tuple-element.28), channel_id=1, source_target_pairs={{0,12},{2,14},{4,8},{6,10},{8,4},{10,6},{12,0},{14,2},{1,13},{3,15... | collective-permute-start | bytes 221192 | tf_op jit(solution)/shard_map/ppermute | solution.py:188
  14.8 1.9 %collective-permute-start.6 = (bf16[144,256]{1,0:T(8,128)(2,1)S(1)}, bf16[144,256]{1,0:T(8,128)(2,1)S(1)}, u32[]{:S(2)}, u32[]{:S(2)}) collective-permute-start(bf16[144,256]{1,0:T(8,128)(2,1)S(1)} %get-tuple-element.29), channel_id=1, source_target_pairs={{0,14},{2,8},{4,10},{6,12},{8,6},{10,0},{12,2},{14,4},{1,15},{3,9}... | collective-permute-start | bytes 221192 | tf_op jit(solution)/shard_map/ppermute | solution.py:188
  17.2 2.5 %collective-permute-done.4.refs_5_ = bf16[144,256]{1,0:T(8,128)(2,1)S(1)} collective-permute-done((bf16[144,256]{1,0:T(8,128)(2,1)S(1)}, bf16[144,256]{1,0:T(8,128)(2,1)S(1)}, u32[]{:S(2)}, u32[]{:S(2)}) %collective-permute-start.4) | collective-permute-done | bytes 73760 | tf_op jit(solution)/shard_map/ppermute | solution.py:188
  22.2 0.7 copy-done.4
  22.9 2.8 %shard_map.87 = (f32[1024,128]{1,0:T(8,128)S(1)}, f32[16,128]{1,0:T(8,128)S(1)}, bf16[1056,128]{1,0:T(8,128)(2,1)S(1)}, bf16[1056,128]{1,0:T(8,128)(2,1)S(1)}, bf16[1056,128]{1,0:T(8,128)(2,1)S(1)}) custom-call(s32[5]{0:T(128)S(1)} %stack.23.pos, s32[1]{0:T(128)} %bitcast.8.count_ref, s32[2,256]{1,0:T(2,128)S(1)} %bitcast.9, ...), custom_call_target="tpu_custom_call" | custom-call | flops 1073741824 | bytes 8388608 | tf_op jit(solution)/shard_map/pallas_call | solution.py:192
  25.7 0.8 %collective-permute-start.15 = (bf16[1056,128]{1,0:T(8,128)(2,1)S(1)}, bf16[1056,128]{1,0:T(8,128)(2,1)S(1)}, u32[]{:S(2)}, u32[]{:S(2)}) collective-permute-start(bf16[1056,128]{1,0:T(8,128)(2,1)S(1)} %get-tuple-element.32), channel_id=1, source_target_pairs={{0,16},{16,32},{32,48},{48,0},{1,17},{17,33},{33,49},{49,1},{2,18}... | collective-permute-start | bytes 811016 | tf_op jit(solution)/shard_map/ppermute | solution.py:212
  26.5 4.3 %collective-permute-start.16 = (bf16[1056,128]{1,0:T(8,128)(2,1)S(1)}, bf16[1056,128]{1,0:T(8,128)(2,1)S(1)}, u32[]{:S(2)}, u32[]{:S(2)}) collective-permute-start(bf16[1056,128]{1,0:T(8,128)(2,1)S(1)} %get-tuple-element.33), channel_id=1, source_target_pairs={{0,32},{16,48},{32,0},{48,16},{1,33},{17,49},{33,1},{49,17},{2,34}... | collective-permute-start | bytes 811016 | tf_op jit(solution)/shard_map/ppermute | solution.py:212
  30.8 1.3 %collective-permute-start.17 = (bf16[1056,128]{1,0:T(8,128)(2,1)S(1)}, bf16[1056,128]{1,0:T(8,128)(2,1)S(1)}, u32[]{:S(2)}, u32[]{:S(2)}) collective-permute-start(bf16[1056,128]{1,0:T(8,128)(2,1)S(1)} %get-tuple-element.34), channel_id=1, source_target_pairs={{0,48},{16,0},{32,16},{48,32},{1,49},{17,1},{33,17},{49,33},{2,50}... | collective-permute-start | bytes 811016 | tf_op jit(solution)/shard_map/ppermute | solution.py:212
  32.5 5.3 %collective-permute-done.16.r2 = bf16[1056,128]{1,0:T(8,128)(2,1)S(1)} collective-permute-done((bf16[1056,128]{1,0:T(8,128)(2,1)S(1)}, bf16[1056,128]{1,0:T(8,128)(2,1)S(1)}, u32[]{:S(2)}, u32[]{:S(2)}) %collective-permute-start.16) | collective-permute-done | bytes 270368 | tf_op jit(solution)/shard_map/ppermute | solution.py:212
  37.8 6.2 %collective-permute-done.17.r3 = bf16[1056,128]{1,0:T(8,128)(2,1)S(1)} collective-permute-done((bf16[1056,128]{1,0:T(8,128)(2,1)S(1)}, bf16[1056,128]{1,0:T(8,128)(2,1)S(1)}, u32[]{:S(2)}, u32[]{:S(2)}) %collective-permute-start.17) | collective-permute-done | bytes 270368 | tf_op jit(solution)/shard_map/ppermute | solution.py:212
  44.0 0.7 shard_map.88
  44.6 4.6 %collective-permute-start.18 = (bf16[288,128]{1,0:T(8,128)(2,1)S(1)}, bf16[288,128]{1,0:T(8,128)(2,1)S(1)}, u32[]{:S(2)}, u32[]{:S(2)}) collective-permute-start(bf16[288,128]{1,0:T(8,128)(2,1)S(1)} %get-tuple-element.37), channel_id=1, source_target_pairs={{0,64},{64,128},{128,192},{192,0},{1,65},{65,129},{129,193},{193,1... | collective-permute-start | bytes 221192 | tf_op jit(solution)/shard_map/ppermute | solution.py:218
  49.2 3.6 %collective-permute-start.19 = (bf16[288,128]{1,0:T(8,128)(2,1)S(1)}, bf16[288,128]{1,0:T(8,128)(2,1)S(1)}, u32[]{:S(2)}, u32[]{:S(2)}) collective-permute-start(bf16[288,128]{1,0:T(8,128)(2,1)S(1)} %get-tuple-element.38), channel_id=1, source_target_pairs={{0,128},{64,192},{128,0},{192,64},{1,129},{65,193},{129,1},{193,65... | collective-permute-start | bytes 221192 | tf_op jit(solution)/shard_map/ppermute | solution.py:218
  52.8 2.4 %collective-permute-start.20 = (bf16[288,128]{1,0:T(8,128)(2,1)S(1)}, bf16[288,128]{1,0:T(8,128)(2,1)S(1)}, u32[]{:S(2)}, u32[]{:S(2)}) collective-permute-start(bf16[288,128]{1,0:T(8,128)(2,1)S(1)} %get-tuple-element.39), channel_id=1, source_target_pairs={{0,192},{64,0},{128,64},{192,128},{1,193},{65,1},{129,65},{193,129... | collective-permute-start | bytes 221192 | tf_op jit(solution)/shard_map/ppermute | solution.py:218
  55.2 3.8 %collective-permute-done.19.r2 = bf16[288,128]{1,0:T(8,128)(2,1)S(1)} collective-permute-done((bf16[288,128]{1,0:T(8,128)(2,1)S(1)}, bf16[288,128]{1,0:T(8,128)(2,1)S(1)}, u32[]{:S(2)}, u32[]{:S(2)}) %collective-permute-start.19) | collective-permute-done | bytes 73760 | tf_op jit(solution)/shard_map/ppermute | solution.py:218
  59.0 0.7 collective-permute-done.20.r3
  59.7 0.7 shard_map.89
  60.5 2.3 %collective-permute-start.27 = (f32[16,128]{1,0:T(8,128)S(1)}, f32[16,128]{1,0:T(8,128)S(1)}, u32[]{:S(2)}, u32[]{:S(2)}) collective-permute-start(f32[16,128]{1,0:T(8,128)S(1)} %get-tuple-element.41.refs_0_), channel_id=1, source_target_pairs={{0,14},{2,8},{4,10},{6,12},{8,6},{10,0},{12,2},{14,4},{1,15},{3,9}... | collective-permute-start | bytes 24584 | tf_op jit(solution)/shard_map/ppermute | solution.py:224
  62.7 3.7 %collective-permute-start.26 = (f32[16,128]{1,0:T(8,128)S(1)}, f32[16,128]{1,0:T(8,128)S(1)}, u32[]{:S(2)}, u32[]{:S(2)}) collective-permute-start(f32[16,128]{1,0:T(8,128)S(1)} %get-tuple-element.41.refs_0_), channel_id=1, source_target_pairs={{0,12},{2,14},{4,8},{6,10},{8,4},{10,6},{12,0},{14,2},{1,13},{3,15... | collective-permute-start | bytes 24584 | tf_op jit(solution)/shard_map/ppermute | solution.py:224
  67.0 4.1 %collective-permute-start.23 = (f32[16,128]{1,0:T(8,128)S(1)}, f32[16,128]{1,0:T(8,128)S(1)}, u32[]{:S(2)}, u32[]{:S(2)}) collective-permute-start(f32[16,128]{1,0:T(8,128)S(1)} %get-tuple-element.41.refs_0_), channel_id=1, source_target_pairs={{0,6},{2,0},{4,2},{6,4},{8,14},{10,8},{12,10},{14,12},{1,7},{3,1},... | collective-permute-start | bytes 24584 | tf_op jit(solution)/shard_map/ppermute | solution.py:224
  71.2 0.9 %collective-permute-start.21 = (f32[16,128]{1,0:T(8,128)S(1)}, f32[16,128]{1,0:T(8,128)S(1)}, u32[]{:S(2)}, u32[]{:S(2)}) collective-permute-start(f32[16,128]{1,0:T(8,128)S(1)} %get-tuple-element.41.refs_0_), channel_id=1, source_target_pairs={{0,2},{2,4},{4,6},{6,0},{8,10},{10,12},{12,14},{14,8},{1,3},{3,5},... | collective-permute-start | bytes 24584 | tf_op jit(solution)/shard_map/ppermute | solution.py:224
  72.5 3.8 %collective-permute-done.22.refs_2_ = f32[16,128]{1,0:T(8,128)S(1)} collective-permute-done((f32[16,128]{1,0:T(8,128)S(1)}, f32[16,128]{1,0:T(8,128)S(1)}, u32[]{:S(2)}, u32[]{:S(2)}) %collective-permute-start.22) | collective-permute-done | bytes 8224 | tf_op jit(solution)/shard_map/ppermute | solution.py:224
  76.3 1.2 %shard_map.90 = f32[128,128]{1,0:T(8,128)} custom-call(s32[5]{0:T(128)S(1)} %stack.23.pos, f32[16,128]{1,0:T(8,128)S(1)} %get-tuple-element.41.refs_0_, f32[16,128]{1,0:T(8,128)S(1)} %collective-permute-done.21.refs_1_, f32[16,128]{1,0:T(8,128)S(1)} %collective-permute-done.22.refs_2_, f32[16,128]{1,0:T(8,128)S(1)} %collective-permute-done.23.refs_3_, ...), custom_call_target="tpu_custom_call" | custom-call | tf_op jit(solution)/shard_map/pallas_call | solution.py:229
  (40 shorter events, 4.1 us)
Async XLA Ops:
  0.7 0.8 %copy-start = (bf16[256,128]{1,0:T(8,128)(2,1)S(1)}, bf16[256,128]{1,0:T(8,128)(2,1)}, u32[]{:S(2)}) copy-start(bf16[256,128]{1,0:T(8,128)(2,1)} %og.1) | copy-start | bytes 196612
  1.6 0.8 %copy-start.1 = (bf16[256,128]{1,0:T(8,128)(2,1)S(1)}, bf16[256,128]{1,0:T(8,128)(2,1)}, u32[]{:S(2)}) copy-start(bf16[256,128]{1,0:T(8,128)(2,1)} %pre.1) | copy-start | bytes 196612
  2.4 0.8 %copy-start.2 = (bf16[256,128]{1,0:T(8,128)(2,1)S(1)}, bf16[256,128]{1,0:T(8,128)(2,1)}, u32[]{:S(2)}) copy-start(bf16[256,128]{1,0:T(8,128)(2,1)} %agg.1) | copy-start | bytes 196612
  3.2 0.8 copy-start.3
  4.8 7.8 %collective-permute-start = (bf16[144,256]{1,0:T(8,128)(2,1)S(1)}, bf16[144,256]{1,0:T(8,128)(2,1)S(1)}, u32[]{:S(2)}, u32[]{:S(2)}) collective-permute-start(bf16[144,256]{1,0:T(8,128)(2,1)S(1)} %get-tuple-element.23), channel_id=1, source_target_pairs={{0,2},{2,4},{4,6},{6,0},{8,10},{10,12},{12,14},{14,8},{1,3},{3,5},... | collective-permute-start | bytes 221192 | tf_op jit(solution)/shard_map/ppermute | solution.py:188
  6.3 8.5 %collective-permute-start.1 = (bf16[144,256]{1,0:T(8,128)(2,1)S(1)}, bf16[144,256]{1,0:T(8,128)(2,1)S(1)}, u32[]{:S(2)}, u32[]{:S(2)}) collective-permute-start(bf16[144,256]{1,0:T(8,128)(2,1)S(1)} %get-tuple-element.24), channel_id=1, source_target_pairs={{0,4},{2,6},{4,0},{6,2},{8,12},{10,14},{12,8},{14,10},{1,5},{3,7},... | collective-permute-start | bytes 221192 | tf_op jit(solution)/shard_map/ppermute | solution.py:188
  9.1 7.6 %collective-permute-start.2 = (bf16[144,256]{1,0:T(8,128)(2,1)S(1)}, bf16[144,256]{1,0:T(8,128)(2,1)S(1)}, u32[]{:S(2)}, u32[]{:S(2)}) collective-permute-start(bf16[144,256]{1,0:T(8,128)(2,1)S(1)} %get-tuple-element.25), channel_id=1, source_target_pairs={{0,6},{2,0},{4,2},{6,4},{8,14},{10,8},{12,10},{14,12},{1,7},{3,1},... | collective-permute-start | bytes 221192 | tf_op jit(solution)/shard_map/ppermute | solution.py:188
  10.5 6.2 %collective-permute-start.3 = (bf16[144,256]{1,0:T(8,128)(2,1)S(1)}, bf16[144,256]{1,0:T(8,128)(2,1)S(1)}, u32[]{:S(2)}, u32[]{:S(2)}) collective-permute-start(bf16[144,256]{1,0:T(8,128)(2,1)S(1)} %get-tuple-element.26), channel_id=1, source_target_pairs={{0,8},{2,10},{4,12},{6,14},{8,0},{10,2},{12,4},{14,6},{1,9},{3,11}... | collective-permute-start | bytes 221192 | tf_op jit(solution)/shard_map/ppermute | solution.py:188
  12.4 7.2 %collective-permute-start.4 = (bf16[144,256]{1,0:T(8,128)(2,1)S(1)}, bf16[144,256]{1,0:T(8,128)(2,1)S(1)}, u32[]{:S(2)}, u32[]{:S(2)}) collective-permute-start(bf16[144,256]{1,0:T(8,128)(2,1)S(1)} %get-tuple-element.27), channel_id=1, source_target_pairs={{0,10},{2,12},{4,14},{6,8},{8,2},{10,4},{12,6},{14,0},{1,11},{3,13... | collective-permute-start | bytes 221192 | tf_op jit(solution)/shard_map/ppermute | solution.py:188
  12.6 7.3 %collective-permute-start.5 = (bf16[144,256]{1,0:T(8,128)(2,1)S(1)}, bf16[144,256]{1,0:T(8,128)(2,1)S(1)}, u32[]{:S(2)}, u32[]{:S(2)}) collective-permute-start(bf16[144,256]{1,0:T(8,128)(2,1)S(1)} %get-tuple-element.28), channel_id=1, source_target_pairs={{0,12},{2,14},{4,8},{6,10},{8,4},{10,6},{12,0},{14,2},{1,13},{3,15... | collective-permute-start | bytes 221192 | tf_op jit(solution)/shard_map/ppermute | solution.py:188
  14.8 5.4 %collective-permute-start.6 = (bf16[144,256]{1,0:T(8,128)(2,1)S(1)}, bf16[144,256]{1,0:T(8,128)(2,1)S(1)}, u32[]{:S(2)}, u32[]{:S(2)}) collective-permute-start(bf16[144,256]{1,0:T(8,128)(2,1)S(1)} %get-tuple-element.29), channel_id=1, source_target_pairs={{0,14},{2,8},{4,10},{6,12},{8,6},{10,0},{12,2},{14,4},{1,15},{3,9}... | collective-permute-start | bytes 221192 | tf_op jit(solution)/shard_map/ppermute | solution.py:188
  16.7 3.7 %collective-permute-start.7 = (bf16[144,256]{1,0:T(8,128)(2,1)S(1)}, bf16[144,256]{1,0:T(8,128)(2,1)S(1)}, u32[]{:S(2)}, u32[]{:S(2)}) collective-permute-start(bf16[144,256]{1,0:T(8,128)(2,1)S(1)} %get-tuple-element.22.refs_0_), channel_id=1, source_target_pairs={{0,1},{1,0},{2,3},{3,2},{4,5},{5,4},{6,7},{7,6},{8,9},{9,8},{10,11... | collective-permute-start | bytes 221192 | tf_op jit(solution)/shard_map/ppermute | solution.py:189
  16.7 4.0 %collective-permute-start.8 = (bf16[144,256]{1,0:T(8,128)(2,1)S(1)}, bf16[144,256]{1,0:T(8,128)(2,1)S(1)}, u32[]{:S(2)}, u32[]{:S(2)}) collective-permute-start(bf16[144,256]{1,0:T(8,128)(2,1)S(1)} %collective-permute-done.refs_1_), channel_id=1, source_target_pairs={{0,1},{1,0},{2,3},{3,2},{4,5},{5,4},{6,7},{7,6},{8,9},{9,8},{10,11... | collective-permute-start | bytes 221192 | tf_op jit(solution)/shard_map/ppermute | solution.py:189
  19.7 1.3 %collective-permute-start.9 = (bf16[144,256]{1,0:T(8,128)(2,1)S(1)}, bf16[144,256]{1,0:T(8,128)(2,1)S(1)}, u32[]{:S(2)}, u32[]{:S(2)}) collective-permute-start(bf16[144,256]{1,0:T(8,128)(2,1)S(1)} %collective-permute-done.1.refs_2_), channel_id=1, source_target_pairs={{0,1},{1,0},{2,3},{3,2},{4,5},{5,4},{6,7},{7,6},{8,9},{9,8},{10,11... | collective-permute-start | bytes 221192 | tf_op jit(solution)/shard_map/ppermute | solution.py:189
  19.9 2.0 %collective-permute-start.10 = (bf16[144,256]{1,0:T(8,128)(2,1)S(1)}, bf16[144,256]{1,0:T(8,128)(2,1)S(1)}, u32[]{:S(2)}, u32[]{:S(2)}) collective-permute-start(bf16[144,256]{1,0:T(8,128)(2,1)S(1)} %collective-permute-done.2.refs_3_), channel_id=1, source_target_pairs={{0,1},{1,0},{2,3},{3,2},{4,5},{5,4},{6,7},{7,6},{8,9},{9,8},{10,11... | collective-permute-start | bytes 221192 | tf_op jit(solution)/shard_map/ppermute | solution.py:189
  20.2 1.7 %collective-permute-start.11 = (bf16[144,256]{1,0:T(8,128)(2,1)S(1)}, bf16[144,256]{1,0:T(8,128)(2,1)S(1)}, u32[]{:S(2)}, u32[]{:S(2)}) collective-permute-start(bf16[144,256]{1,0:T(8,128)(2,1)S(1)} %collective-permute-done.3.refs_4_), channel_id=1, source_target_pairs={{0,1},{1,0},{2,3},{3,2},{4,5},{5,4},{6,7},{7,6},{8,9},{9,8},{10,11... | collective-permute-start | bytes 221192 | tf_op jit(solution)/shard_map/ppermute | solution.py:189
  20.4 1.5 %collective-permute-start.12 = (bf16[144,256]{1,0:T(8,128)(2,1)S(1)}, bf16[144,256]{1,0:T(8,128)(2,1)S(1)}, u32[]{:S(2)}, u32[]{:S(2)}) collective-permute-start(bf16[144,256]{1,0:T(8,128)(2,1)S(1)} %collective-permute-done.4.refs_5_), channel_id=1, source_target_pairs={{0,1},{1,0},{2,3},{3,2},{4,5},{5,4},{6,7},{7,6},{8,9},{9,8},{10,11... | collective-permute-start | bytes 221192 | tf_op jit(solution)/shard_map/ppermute | solution.py:189
  20.7 1.3 %collective-permute-start.13 = (bf16[144,256]{1,0:T(8,128)(2,1)S(1)}, bf16[144,256]{1,0:T(8,128)(2,1)S(1)}, u32[]{:S(2)}, u32[]{:S(2)}) collective-permute-start(bf16[144,256]{1,0:T(8,128)(2,1)S(1)} %collective-permute-done.5.refs_6_), channel_id=1, source_target_pairs={{0,1},{1,0},{2,3},{3,2},{4,5},{5,4},{6,7},{7,6},{8,9},{9,8},{10,11... | collective-permute-start | bytes 221192 | tf_op jit(solution)/shard_map/ppermute | solution.py:189
  20.9 1.3 %collective-permute-start.14 = (bf16[144,256]{1,0:T(8,128)(2,1)S(1)}, bf16[144,256]{1,0:T(8,128)(2,1)S(1)}, u32[]{:S(2)}, u32[]{:S(2)}) collective-permute-start(bf16[144,256]{1,0:T(8,128)(2,1)S(1)} %collective-permute-done.6.refs_7_), channel_id=1, source_target_pairs={{0,1},{1,0},{2,3},{3,2},{4,5},{5,4},{6,7},{7,6},{8,9},{9,8},{10,11... | collective-permute-start | bytes 221192 | tf_op jit(solution)/shard_map/ppermute | solution.py:189
  25.7 6.8 %collective-permute-start.15 = (bf16[1056,128]{1,0:T(8,128)(2,1)S(1)}, bf16[1056,128]{1,0:T(8,128)(2,1)S(1)}, u32[]{:S(2)}, u32[]{:S(2)}) collective-permute-start(bf16[1056,128]{1,0:T(8,128)(2,1)S(1)} %get-tuple-element.32), channel_id=1, source_target_pairs={{0,16},{16,32},{32,48},{48,0},{1,17},{17,33},{33,49},{49,1},{2,18}... | collective-permute-start | bytes 811016 | tf_op jit(solution)/shard_map/ppermute | solution.py:212
  26.5 11.3 %collective-permute-start.16 = (bf16[1056,128]{1,0:T(8,128)(2,1)S(1)}, bf16[1056,128]{1,0:T(8,128)(2,1)S(1)}, u32[]{:S(2)}, u32[]{:S(2)}) collective-permute-start(bf16[1056,128]{1,0:T(8,128)(2,1)S(1)} %get-tuple-element.33), channel_id=1, source_target_pairs={{0,32},{16,48},{32,0},{48,16},{1,33},{17,49},{33,1},{49,17},{2,34}... | collective-permute-start | bytes 811016 | tf_op jit(solution)/shard_map/ppermute | solution.py:212
  30.8 13.1 %collective-permute-start.17 = (bf16[1056,128]{1,0:T(8,128)(2,1)S(1)}, bf16[1056,128]{1,0:T(8,128)(2,1)S(1)}, u32[]{:S(2)}, u32[]{:S(2)}) collective-permute-start(bf16[1056,128]{1,0:T(8,128)(2,1)S(1)} %get-tuple-element.34), channel_id=1, source_target_pairs={{0,48},{16,0},{32,16},{48,32},{1,49},{17,1},{33,17},{49,33},{2,50}... | collective-permute-start | bytes 811016 | tf_op jit(solution)/shard_map/ppermute | solution.py:212
  44.6 10.6 %collective-permute-start.18 = (bf16[288,128]{1,0:T(8,128)(2,1)S(1)}, bf16[288,128]{1,0:T(8,128)(2,1)S(1)}, u32[]{:S(2)}, u32[]{:S(2)}) collective-permute-start(bf16[288,128]{1,0:T(8,128)(2,1)S(1)} %get-tuple-element.37), channel_id=1, source_target_pairs={{0,64},{64,128},{128,192},{192,0},{1,65},{65,129},{129,193},{193,1... | collective-permute-start | bytes 221192 | tf_op jit(solution)/shard_map/ppermute | solution.py:218
  49.2 9.8 %collective-permute-start.19 = (bf16[288,128]{1,0:T(8,128)(2,1)S(1)}, bf16[288,128]{1,0:T(8,128)(2,1)S(1)}, u32[]{:S(2)}, u32[]{:S(2)}) collective-permute-start(bf16[288,128]{1,0:T(8,128)(2,1)S(1)} %get-tuple-element.38), channel_id=1, source_target_pairs={{0,128},{64,192},{128,0},{192,64},{1,129},{65,193},{129,1},{193,65... | collective-permute-start | bytes 221192 | tf_op jit(solution)/shard_map/ppermute | solution.py:218
  52.8 6.9 %collective-permute-start.20 = (bf16[288,128]{1,0:T(8,128)(2,1)S(1)}, bf16[288,128]{1,0:T(8,128)(2,1)S(1)}, u32[]{:S(2)}, u32[]{:S(2)}) collective-permute-start(bf16[288,128]{1,0:T(8,128)(2,1)S(1)} %get-tuple-element.39), channel_id=1, source_target_pairs={{0,192},{64,0},{128,64},{192,128},{1,193},{65,1},{129,65},{193,129... | collective-permute-start | bytes 221192 | tf_op jit(solution)/shard_map/ppermute | solution.py:218
  60.5 10.7 %collective-permute-start.27 = (f32[16,128]{1,0:T(8,128)S(1)}, f32[16,128]{1,0:T(8,128)S(1)}, u32[]{:S(2)}, u32[]{:S(2)}) collective-permute-start(f32[16,128]{1,0:T(8,128)S(1)} %get-tuple-element.41.refs_0_), channel_id=1, source_target_pairs={{0,14},{2,8},{4,10},{6,12},{8,6},{10,0},{12,2},{14,4},{1,15},{3,9}... | collective-permute-start | bytes 24584 | tf_op jit(solution)/shard_map/ppermute | solution.py:224
  62.7 8.4 %collective-permute-start.26 = (f32[16,128]{1,0:T(8,128)S(1)}, f32[16,128]{1,0:T(8,128)S(1)}, u32[]{:S(2)}, u32[]{:S(2)}) collective-permute-start(f32[16,128]{1,0:T(8,128)S(1)} %get-tuple-element.41.refs_0_), channel_id=1, source_target_pairs={{0,12},{2,14},{4,8},{6,10},{8,4},{10,6},{12,0},{14,2},{1,13},{3,15... | collective-permute-start | bytes 24584 | tf_op jit(solution)/shard_map/ppermute | solution.py:224
  66.4 5.8 %collective-permute-start.25 = (f32[16,128]{1,0:T(8,128)S(1)}, f32[16,128]{1,0:T(8,128)S(1)}, u32[]{:S(2)}, u32[]{:S(2)}) collective-permute-start(f32[16,128]{1,0:T(8,128)S(1)} %get-tuple-element.41.refs_0_), channel_id=1, source_target_pairs={{0,10},{2,12},{4,14},{6,8},{8,2},{10,4},{12,6},{14,0},{1,11},{3,13... | collective-permute-start | bytes 24584 | tf_op jit(solution)/shard_map/ppermute | solution.py:224
  67.0 5.2 %collective-permute-start.24 = (f32[16,128]{1,0:T(8,128)S(1)}, f32[16,128]{1,0:T(8,128)S(1)}, u32[]{:S(2)}, u32[]{:S(2)}) collective-permute-start(f32[16,128]{1,0:T(8,128)S(1)} %get-tuple-element.41.refs_0_), channel_id=1, source_target_pairs={{0,8},{2,10},{4,12},{6,14},{8,0},{10,2},{12,4},{14,6},{1,9},{3,11}... | collective-permute-start | bytes 24584 | tf_op jit(solution)/shard_map/ppermute | solution.py:224
  67.0 5.5 %collective-permute-start.23 = (f32[16,128]{1,0:T(8,128)S(1)}, f32[16,128]{1,0:T(8,128)S(1)}, u32[]{:S(2)}, u32[]{:S(2)}) collective-permute-start(f32[16,128]{1,0:T(8,128)S(1)} %get-tuple-element.41.refs_0_), channel_id=1, source_target_pairs={{0,6},{2,0},{4,2},{6,4},{8,14},{10,8},{12,10},{14,12},{1,7},{3,1},... | collective-permute-start | bytes 24584 | tf_op jit(solution)/shard_map/ppermute | solution.py:224
  71.1 5.2 %collective-permute-start.22 = (f32[16,128]{1,0:T(8,128)S(1)}, f32[16,128]{1,0:T(8,128)S(1)}, u32[]{:S(2)}, u32[]{:S(2)}) collective-permute-start(f32[16,128]{1,0:T(8,128)S(1)} %get-tuple-element.41.refs_0_), channel_id=1, source_target_pairs={{0,4},{2,6},{4,0},{6,2},{8,12},{10,14},{12,8},{14,10},{1,5},{3,7},... | collective-permute-start | bytes 24584 | tf_op jit(solution)/shard_map/ppermute | solution.py:224
  71.2 5.2 %collective-permute-start.21 = (f32[16,128]{1,0:T(8,128)S(1)}, f32[16,128]{1,0:T(8,128)S(1)}, u32[]{:S(2)}, u32[]{:S(2)}) collective-permute-start(f32[16,128]{1,0:T(8,128)S(1)} %get-tuple-element.41.refs_0_), channel_id=1, source_target_pairs={{0,2},{2,4},{4,6},{6,0},{8,10},{10,12},{12,14},{14,8},{1,3},{3,5},... | collective-permute-start | bytes 24584 | tf_op jit(solution)/shard_map/ppermute | solution.py:224
  (1 other events, 0.7 us)

commit v2 on v1

v2 whole, which is shorter than its diff:
```python
import functools
import itertools

import jax
import jax.numpy as jnp
from jax import lax
from jax.experimental import pallas as pl
from jax.experimental.pallas import tpu as pltpu
from jax.sharding import Mesh, PartitionSpec as P

bf16 = jnp.bfloat16
f32 = jnp.float32
i32 = jnp.int32
T = 128
ROWS = ("zh", "y")
COLS = ("zl", "x", "core")
BLOCKS = 32
SLOTS = 256
PLACES = 384
PART = 32
UNROLL = 4
LIMIT = 16 * 1024 * 1024


def spec(space=pltpu.VMEM):
    return pl.BlockSpec(memory_space=space)


def split_parts(value):
    high = value.astype(bf16)
    low = (value - high.astype(f32)).astype(bf16)
    return high, low


def ring_sum(own, received):
    return (own + received[1]) + (received[0] + received[2])


def local_kernel(inputs, message):
    n = (inputs.shape[0] - T) // 3
    og, pre, agg = (inputs[pl.ds(i * n, n), :] for i in range(3))
    weight = inputs[3 * n :, :]
    grad_pre = jnp.where(pre > 0, og, jnp.zeros_like(og))
    message[0:T, :] = lax.dot_general(
        weight, grad_pre, (((1,), (1,)), ((), ())), preferred_element_type=f32
    ).astype(bf16)
    partial = lax.dot_general(
        agg, grad_pre, (((0,), (0,)), ((), ())), preferred_element_type=f32
    )
    high, low = split_parts(partial)
    message[T : 2 * T, 0:T] = high
    message[T : 2 * T, T : 2 * T] = low


def chip_kernel(pos, own, other, message):
    core = pos[4]
    message[pl.ds(pl.multiple_of(core * T, T), T), :] = own[0:T, :]
    message[pl.ds(pl.multiple_of((1 - core) * T, T), T), :] = other[0:T, :]
    sums = [m[T : 2 * T, 0:T].astype(f32) + m[T : 2 * T, T : 2 * T].astype(f32) for m in (own, other)]
    total = (sums[0] + sums[1]).astype(bf16)
    message[2 * T : 2 * T + 64, 0:T] = total[0:64, :]
    message[2 * T : 2 * T + 64, T : 2 * T] = total[64:T, :]


def order_kernel(count_ref, coords_hbm, tiles_hbm, out, tiles, coords, listed, sems):
    fetches = [
        pltpu.make_async_copy(tiles_hbm.at[part], tiles.at[part], sems.at[1 + i])
        for i, part in enumerate(pl.ds(g * PART, PART) for g in range(SLOTS // PART))
    ]
    fetch_coords = pltpu.make_async_copy(coords_hbm, coords, sems.at[0])
    fetch_coords.start()
    for fetch in fetches:
        fetch.start()
    fetch_coords.wait()
    count = count_ref[0]
    shape = (SLOTS, SLOTS)
    at_k = lax.broadcasted_iota(i32, shape, 0)
    at_j = lax.broadcasted_iota(i32, shape, 1)
    same = at_k == at_j
    row_j = jnp.broadcast_to(coords[0:1, :], shape)
    col_j = jnp.broadcast_to(coords[1:2, :], shape)

    def down(value_j):
        return jnp.sum(jnp.where(same, value_j, 0), axis=1, keepdims=True)

    def across(value_k):
        return jnp.sum(jnp.where(same, value_k, 0), axis=0, keepdims=True)

    row_k, col_k = down(row_j), down(col_j)
    live_j = at_j < count
    before = live_j & (col_j == col_k) & (at_j < at_k)
    rank_k = jnp.sum(before.astype(i32), axis=1, keepdims=True)
    opens_j = live_j & ((across(rank_k) & 1) == 0)
    pair_k = jnp.sum((opens_j & (col_j < col_k)).astype(i32), axis=1, keepdims=True) + (rank_k >> 1)
    slot_k = lax.broadcasted_iota(i32, (SLOTS, 1), 0)
    place_k = jnp.where(slot_k < count, 2 * pair_k + (rank_k & 1), -1)
    code_k = slot_k + (row_k << 8) + (col_k << 16)
    places = lax.broadcasted_iota(i32, (SLOTS, PLACES), 1)
    hit = places == place_k
    code = jnp.sum(jnp.where(hit, code_k, 0), axis=0, keepdims=True)
    found = jnp.sum(hit.astype(i32), axis=0, keepdims=True)
    code = jnp.where(found > 0, code, BLOCKS << 8)
    pairs = jnp.sum(opens_j[0:1, :].astype(i32), axis=1, keepdims=True)
    last = lax.broadcasted_iota(i32, (1, PLACES), 1) == PLACES - 1
    listed[...] = jnp.where(last, pairs, code)
    hand_over = pltpu.make_async_copy(listed, out, sems.at[0])
    hand_over.start()
    hand_over.wait()
    for fetch in fetches:
        fetch.wait()


def tile_kernel(pos, order, *refs):
    mine, got, swapped = refs[0], refs[1:5], refs[5:9]
    tiles = refs[9]
    keep, keep_w, sends = refs[10], refs[11], refs[12:15]
    grads, acc, parts = refs[15:]
    y, zl, x, core = pos[1], pos[2], pos[3], pos[4]

    arrived = [(got[k], core, k) for k in range(4)]
    arrived += [(swapped[k], 1 - core, k) for k in range(4)]
    arrived += [(mine, 0, 0)]
    for message, dz, dx in arrived:
        chip = ((zl + 2 - dz) % 2) * 4 + (x + 4 - dx) % 4
        for c in range(2):
            for h in range(2):
                grads[chip * 4 + 2 * c + h] = message[c * T : (c + 1) * T, h * T : (h + 1) * T]
        parts[chip] = message[2 * T : 2 * T + 64, :]
    grads[BLOCKS] = jnp.zeros((T, T), bf16)
    acc[...] = jnp.zeros_like(acc)
    pairs = order[0, PLACES - 1]

    @pl.loop(0, (pairs + UNROLL - 1) // UNROLL)
    def _(group):
        for u in range(UNROLL):
            pair = group * UNROLL + u
            first, second = order[0, 2 * pair], order[0, 2 * pair + 1]
            left = jnp.concatenate([grads[(first >> 8) & 63], grads[(second >> 8) & 63]], axis=1)
            right = jnp.concatenate([tiles[first & 255], tiles[second & 255]], axis=0)
            acc[first >> 16] += jnp.dot(left, right, preferred_element_type=f32)

    total = parts[0].astype(f32)
    for chip in range(1, 8):
        total += parts[chip].astype(f32)
    rounded = total.astype(bf16)
    for d in range(4):
        for zh in range(4):
            for h in range(2):
                q = (zh * 4 + (y + d) % 4) * 2 + h
                rows = pl.ds((zh * 2 + h) * T, T)
                if d == 0:
                    keep[rows, :] = acc[q]
                else:
                    sends[d - 1][rows, :] = acc[q].astype(bf16)
        if d:
            sends[d - 1][1024:1088, :] = rounded[:, 0:T]
            sends[d - 1][1088:1152, :] = rounded[:, T : 2 * T]
    keep_w[0:64, :] = rounded[:, 0:T]
    keep_w[64:T, :] = rounded[:, T : 2 * T]


def y_kernel(pos, keep, keep_w, r1, r2, r3, keep_z, keep_zw, s1, s2, s3):
    zh_me = pos[0]
    parts = [r[1024:1152, :].astype(f32) for r in (r1, r2, r3)]
    rounded = ring_sum(keep_w[...].astype(f32), parts).astype(bf16)
    keep_zw[...] = rounded
    for d, out in enumerate((keep_z, s1, s2, s3)):
        rows = pl.ds(pl.multiple_of(((zh_me + d) % 4) * 256, 256), 256)
        total = keep[rows, :]
        for r in (r1, r2, r3):
            total += r[rows, :].astype(f32)
        if d == 0:
            out[...] = total
        else:
            out[0:256, :] = total.astype(bf16)
            out[256:384, :] = rounded


def z_kernel(scale, keep_z, keep_zw, r1, r2, r3, out, weight_out):
    parts = [r[256:384, :].astype(f32) for r in (r1, r2, r3)]
    weight_out[...] = ring_sum(keep_zw[...].astype(f32), parts) * scale
    for h in range(2):
        rows = pl.ds(h * T, T)
        total = keep_z[rows, :]
        for r in (r1, r2, r3):
            total += r[rows, :].astype(f32)
        out[rows, :] = total.T.astype(bf16)


def call(kernel, out_shape, in_specs, scratch=(), cost=None, out_specs=None):
    return pl.pallas_call(
        kernel,
        out_shape=out_shape,
        in_specs=in_specs,
        out_specs=out_specs or jax.tree.map(lambda _: spec(), out_shape),
        scratch_shapes=list(scratch),
        compiler_params=pltpu.CompilerParams(vmem_limit_bytes=LIMIT),
        cost_estimate=cost,
    )


def struct(*shape, dtype=bf16):
    return jax.ShapeDtypeStruct(shape, dtype)


def chip_perm(k):
    pairs = []
    for z, x, c in itertools.product(range(2), range(4), range(2)):
        if c or k:
            pairs.append(((z * 4 + x) * 2 + c, (((z + c) % 2) * 4 + (x + k) % 4) * 2 + c))
    return pairs


def body(out_grad, preact, aggregated, weight, tiles, tile_coords, tile_count):
    smem, vmem, hbm = spec(pltpu.SMEM), spec(), spec(pltpu.HBM)
    nodes = out_grad.shape[0]
    pos = jnp.stack([lax.axis_index(a) for a in ROWS + COLS]).astype(i32)
    swap = [(0, 1), (1, 0)]
    inputs = jnp.concatenate([out_grad, preact, aggregated, weight], 0)
    local = call(local_kernel, struct(2 * T, nodes), [vmem])(inputs)
    mine = call(chip_kernel, struct(2 * T + 64, nodes), [smem, vmem, vmem])(
        pos, local, lax.ppermute(local, "core", swap)
    )
    order, held = call(
        order_kernel,
        [pltpu.SMEM((1, PLACES), i32), pltpu.VMEM((SLOTS, T, T), bf16)],
        [smem, hbm, hbm],
        [pltpu.VMEM((2, SLOTS), i32), pltpu.VMEM((1, PLACES), i32), pltpu.SemaphoreType.DMA((1 + SLOTS // PART,))],
        pl.CostEstimate(flops=0, bytes_accessed=2 * SLOTS * T * T * 2, transcendentals=0),
        (smem, vmem),
    )(
        tile_count.reshape(1),
        pltpu.with_memory_space_constraint(tile_coords.reshape(2, SLOTS), pltpu.HBM),
        pltpu.with_memory_space_constraint(tiles.reshape(SLOTS, T, T), pltpu.HBM),
    )
    got = [lax.ppermute(mine, COLS, chip_perm(k)) for k in range(4)]
    swapped = []
    for k in range(4):
        ready, _ = lax.optimization_barrier((got[k], order))
        swapped.append(lax.ppermute(ready, "core", swap))
    keep, keep_w, *sends = call(
        tile_kernel,
        [struct(1024, T, dtype=f32), struct(T, T)] + [struct(1152, T)] * 3,
        [smem] * 2 + [vmem] * 10,
        [
            pltpu.VMEM((BLOCKS + 1, T, T), bf16),
            pltpu.VMEM((BLOCKS, T, T), f32),
            pltpu.VMEM((8, 64, 2 * T), bf16),
        ],
        pl.CostEstimate(flops=SLOTS * 2 * T**3, bytes_accessed=SLOTS * T * T * 2, transcendentals=0),
    )(pos, order, mine, *got, *swapped, held)
    turn = lambda d: [(i, (i + d) % 4) for i in range(4)]
    got = [lax.ppermute(s, "y", turn(d)) for d, s in zip((1, 2, 3), sends)]
    keep_z, keep_zw, *sends = call(
        y_kernel,
        [struct(256, T, dtype=f32), struct(T, T)] + [struct(384, T)] * 3,
        [smem] + [vmem] * 5,
    )(pos, keep, keep_w, *got)
    got = [lax.ppermute(s, "zh", turn(d)) for d, s in zip((1, 2, 3), sends)]
    devices = 1
    for a in ROWS + COLS:
        devices *= lax.axis_size(a)
    scale = 1.0 / (nodes * devices) ** 0.5
    input_grad, weight_grad = call(
        functools.partial(z_kernel, scale),
        [struct(nodes, T), struct(T, T, dtype=f32)],
        [vmem] * 5,
    )(keep_z, keep_zw, *got)
    return input_grad, weight_grad


def solution(mesh):
    fine = Mesh(mesh.devices.reshape(4, 4, 2, 4, 2), ROWS + COLS)
    every = ROWS + COLS
    return jax.shard_map(
        body,
        mesh=fine,
        in_specs=(
            P(every, None),
            P(every, None),
            P(every, None),
            P(),
            P(ROWS, COLS, None, None, None),
            P(ROWS, COLS, None, None),
            P(ROWS, COLS),
        ),
        out_specs=(P(every, None), P()),
        check_vma=False,
    )
```

time: 78.2 us -> 63.4 us (0.81)
  the two profiles are of different devices: /device:TPU:24 before, /device:TPU:1 now
where the time goes in v2:
time: 63.4 us; the launch traced here: 63.8 us
  starting transfers between devices  24.6 us (39%)
  waiting for transfers between devices  23.7 us (37%)
  Pallas kernels  13.1 us (21%)
  between operations  1.36 us (2%)
  other arithmetic  0.94 us (1%)
    ppermute x3, waiting for transfers between devices, body(): got = [lax.ppermute(s, 'y', turn(d)) for d, s in zip((1, 2, 3), sends)]  12.8 us
    ppermute x3, starting transfers between devices, body(): got = [lax.ppermute(s, 'zh', turn(d)) for d, s in zip((1, 2, 3), sends)]  9.1 us
    ppermute x3, waiting for transfers between devices, body(): got = [lax.ppermute(s, 'zh', turn(d)) for d, s in zip((1, 2, 3), sends)]  8.23 us
    pallas_call x1, Pallas kernels, body(): call(tile_kernel, [struct(1024, T, dtype=f32), struct(T, T)] + [struct(11...  7.36 us
    ppermute x4, starting transfers between devices, body(): got = [lax.ppermute(mine, COLS, chip_perm(k)) for k in range(4)]  6.11 us
    pallas_call x1, Pallas kernels, body(): call(order_kernel, [pltpu.SMEM((1, PLACES), i32), pltpu.VMEM((SLOTS, T, T...  3.5 us
    ppermute x4, starting transfers between devices, body(): swapped.append(lax.ppermute(ready, 'core', swap))  3.36 us
    ppermute x1, starting transfers between devices, body(): lax.ppermute(local, 'core', swap)  3.33 us
  transfers between devices with their start and end apart: 15, of which 13 were waited for; matrix products, arithmetic and copies ran while one was open for 0% of the time, Pallas kernels for 5%

profile of v2, /device:TPU:1, one launch (start us, length us, event | category | flops | bytes accessed | tf_op | source)
XLA Modules:
  0.0 63.8 jit_solution(16718772419143863622)
XLA Ops:
  0.6 0.9 %pad_maximum_fusion.inputs = bf16[896,128]{1,0:T(8,128)(2,1)S(1)} fusion(bf16[128,128]{1,0:T(8,128)(2,1)} %param.10, bf16[256,128]{1,0:T(8,128)(2,1)} %param.9, bf16[256,128]{1,0:T(8,128)(2,1)} %param.8, bf16[256,128]{1,0:T(8,128)(2,1)} %param.7), kind=kLoop, calls=%fused_computation | loop fusion | flops 917504 | bytes 458752 | tf_op jit(solution)/shard_map/concatenate | solution.py:219
  1.6 0.2 shard_map.87.own
  1.8 3.3 %collective-permute-start = (bf16[256,256]{1,0:T(8,128)(2,1)S(1)}, bf16[256,256]{1,0:T(8,128)(2,1)S(1)}, u32[]{:S(2)}, u32[]{:S(2)}) collective-permute-start(bf16[256,256]{1,0:T(8,128)(2,1)S(1)} %shard_map.87.own), channel_id=1, source_target_pairs={{0,1},{1,0},{2,3},{3,2},{4,5},{5,4},{6,7},{7,6},{8,9},{9,8},{10,11... | collective-permute-start | bytes 393224 | tf_op jit(solution)/shard_map/ppermute | solution.py:222
  5.1 0.1 stack.23.pos
  5.2 0.9 %collective-permute-done.other = bf16[256,256]{1,0:T(8,128)(2,1)S(1)} collective-permute-done((bf16[256,256]{1,0:T(8,128)(2,1)S(1)}, bf16[256,256]{1,0:T(8,128)(2,1)S(1)}, u32[]{:S(2)}, u32[]{:S(2)}) %collective-permute-start) | collective-permute-done | bytes 131104 | tf_op jit(solution)/shard_map/ppermute | solution.py:222
  6.1 0.6 shard_map.88.refs_0_
  6.7 2.2 %collective-permute-start.4 = (bf16[320,256]{1,0:T(8,128)(2,1)S(1)}, bf16[320,256]{1,0:T(8,128)(2,1)S(1)}, u32[]{:S(2)}, u32[]{:S(2)}) collective-permute-start(bf16[320,256]{1,0:T(8,128)(2,1)S(1)} %shard_map.88.refs_0_), channel_id=1, source_target_pairs={{0,6},{1,15},{2,0},{3,9},{4,2},{5,11},{6,4},{7,13},{8,14},{9,7},{1... | collective-permute-start | bytes 491528 | tf_op jit(solution)/shard_map/ppermute | solution.py:236
  8.9 0.4 collective-permute-start.3
  9.2 1.7 %collective-permute-start.2 = (bf16[320,256]{1,0:T(8,128)(2,1)S(1)}, bf16[320,256]{1,0:T(8,128)(2,1)S(1)}, u32[]{:S(2)}, u32[]{:S(2)}) collective-permute-start(bf16[320,256]{1,0:T(8,128)(2,1)S(1)} %shard_map.88.refs_0_), channel_id=1, source_target_pairs={{0,2},{1,11},{2,4},{3,13},{4,6},{5,15},{6,0},{7,9},{8,10},{9,3},{1... | collective-permute-start | bytes 491528 | tf_op jit(solution)/shard_map/ppermute | solution.py:236
  10.9 1.9 %collective-permute-start.1 = (bf16[320,256]{1,0:T(8,128)(2,1)S(1)}, bf16[320,256]{1,0:T(8,128)(2,1)S(1)}, u32[]{:S(2)}, u32[]{:S(2)}) collective-permute-start(bf16[320,256]{1,0:T(8,128)(2,1)S(1)} %shard_map.88.refs_0_), channel_id=1, source_target_pairs={{1,9},{3,11},{5,13},{7,15},{9,1},{11,3},{13,5},{15,7},{17,25},{19,... | collective-permute-start | bytes 491528 | tf_op jit(solution)/shard_map/ppermute | solution.py:236
  13.4 3.5 %shard_map.86 = (s32[1,384]{1,0:T(1,128)S(4)}, bf16[256,128,128]{2,1,0:T(8,128)(2,1)S(1)}) custom-call(s32[1]{0:T(128)} %bitcast.8.count_ref, s32[2,256]{1,0:T(2,128)} %bitcast.10, bf16[256,128,128]{2,1,0:T(8,128)(2,1)} %bitcast.9), custom_call_target="tpu_custom_call" | custom-call | bytes 16777216 | tf_op jit(solution)/shard_map/pallas_call | solution.py:224
  17.0 0.1 collective-permute-done.3.refs_3_
  17.1 0.3 collective-permute-done.2.refs_2_
  17.4 2.8 %collective-permute-start.5 = (bf16[320,256]{1,0:T(8,128)(2,1)S(1)}, bf16[320,256]{1,0:T(8,128)(2,1)S(1)}, u32[]{:S(2)}, u32[]{:S(2)}) collective-permute-start(bf16[320,256]{1,0:T(8,128)(2,1)S(1)} %collective-permute-done.1.refs_1_), channel_id=1, source_target_pairs={{0,1},{1,0},{2,3},{3,2},{4,5},{5,4},{6,7},{7,6},{8,9},{9,8},{10,11... | collective-permute-start | bytes 491528 | tf_op jit(solution)/shard_map/ppermute | solution.py:240
  20.2 0.5 collective-permute-start.7
  20.8 0.5 collective-permute-done.5.refs_5_
  21.3 0.4 collective-permute-done.6.refs_6_
  21.6 0.2 collective-permute-done.7.refs_7_
  21.9 0.3 collective-permute-done.8.refs_8_
  22.1 7.4 %shard_map.89 = (f32[1024,128]{1,0:T(8,128)S(1)}, bf16[128,128]{1,0:T(8,128)(2,1)S(1)}, bf16[1152,128]{1,0:T(8,128)(2,1)S(1)}, bf16[1152,128]{1,0:T(8,128)(2,1)S(1)}, bf16[1152,128]{1,0:T(8,128)(2,1)S(1)}) custom-call(s32[5]{0:T(128)S(1)} %stack.23.pos, s32[1,384]{1,0:T(1,128)S(4)} %get-tuple-element.18.order, bf16[320,256]{1,0:T(8,128)(2,1)S(1)} %shard_map.88.refs_0_, ...), custom_call_target="tpu_custom_call" | custom-call | flops 1073741824 | bytes 8388608 | tf_op jit(solution)/shard_map/pallas_call | solution.py:241
  29.6 1.2 %collective-permute-start.10 = (bf16[1152,128]{1,0:T(8,128)(2,1)S(1)}, bf16[1152,128]{1,0:T(8,128)(2,1)S(1)}, u32[]{:S(2)}, u32[]{:S(2)}) collective-permute-start(bf16[1152,128]{1,0:T(8,128)(2,1)S(1)} %get-tuple-element.27), channel_id=1, source_target_pairs={{0,32},{16,48},{32,0},{48,16},{1,33},{17,49},{33,1},{49,17},{2,34}... | collective-permute-start | bytes 884744 | tf_op jit(solution)/shard_map/ppermute | solution.py:253
  30.8 1.5 %collective-permute-start.11 = (bf16[1152,128]{1,0:T(8,128)(2,1)S(1)}, bf16[1152,128]{1,0:T(8,128)(2,1)S(1)}, u32[]{:S(2)}, u32[]{:S(2)}) collective-permute-start(bf16[1152,128]{1,0:T(8,128)(2,1)S(1)} %get-tuple-element.28), channel_id=1, source_target_pairs={{0,48},{16,0},{32,16},{48,32},{1,49},{17,1},{33,17},{49,33},{2,50}... | collective-permute-start | bytes 884744 | tf_op jit(solution)/shard_map/ppermute | solution.py:253
  32.3 6.3 %collective-permute-done.9.r1 = bf16[1152,128]{1,0:T(8,128)(2,1)S(1)} collective-permute-done((bf16[1152,128]{1,0:T(8,128)(2,1)S(1)}, bf16[1152,128]{1,0:T(8,128)(2,1)S(1)}, u32[]{:S(2)}, u32[]{:S(2)}) %collective-permute-start.9) | collective-permute-done | bytes 294944 | tf_op jit(solution)/shard_map/ppermute | solution.py:253
  38.6 4.9 %collective-permute-done.10.r2 = bf16[1152,128]{1,0:T(8,128)(2,1)S(1)} collective-permute-done((bf16[1152,128]{1,0:T(8,128)(2,1)S(1)}, bf16[1152,128]{1,0:T(8,128)(2,1)S(1)}, u32[]{:S(2)}, u32[]{:S(2)}) %collective-permute-start.10) | collective-permute-done | bytes 294944 | tf_op jit(solution)/shard_map/ppermute | solution.py:253
  43.5 1.6 %collective-permute-done.11.r3 = bf16[1152,128]{1,0:T(8,128)(2,1)S(1)} collective-permute-done((bf16[1152,128]{1,0:T(8,128)(2,1)S(1)}, bf16[1152,128]{1,0:T(8,128)(2,1)S(1)}, u32[]{:S(2)}, u32[]{:S(2)}) %collective-permute-start.11) | collective-permute-done | bytes 294944 | tf_op jit(solution)/shard_map/ppermute | solution.py:253
  45.0 0.7 %shard_map.90 = (f32[256,128]{1,0:T(8,128)S(1)}, bf16[128,128]{1,0:T(8,128)(2,1)S(1)}, bf16[384,128]{1,0:T(8,128)(2,1)S(1)}, bf16[384,128]{1,0:T(8,128)(2,1)S(1)}, bf16[384,128]{1,0:T(8,128)(2,1)S(1)}) custom-call(s32[5]{0:T(128)S(1)} %stack.23.pos, f32[1024,128]{1,0:T(8,128)S(1)} %get-tuple-element.24.keep, bf16[128,128]{1,0:T(8,128)(2,1)S(1)} %get-tuple-element.25.keep_w, ...), custom_call_target="tpu_custom_call" | custom-call | tf_op jit(solution)/shard_map/pallas_call | solution.py:254
  45.8 8.6 %collective-permute-start.13 = (bf16[384,128]{1,0:T(8,128)(2,1)S(1)}, bf16[384,128]{1,0:T(8,128)(2,1)S(1)}, u32[]{:S(2)}, u32[]{:S(2)}) collective-permute-start(bf16[384,128]{1,0:T(8,128)(2,1)S(1)} %get-tuple-element.32), channel_id=1, source_target_pairs={{0,128},{64,192},{128,0},{192,64},{1,129},{65,193},{129,1},{193,65... | collective-permute-start | bytes 294920 | tf_op jit(solution)/shard_map/ppermute | solution.py:259
  54.5 0.4 collective-permute-start.14
  54.8 3.2 %collective-permute-done.12.r1 = bf16[384,128]{1,0:T(8,128)(2,1)S(1)} collective-permute-done((bf16[384,128]{1,0:T(8,128)(2,1)S(1)}, bf16[384,128]{1,0:T(8,128)(2,1)S(1)}, u32[]{:S(2)}, u32[]{:S(2)}) %collective-permute-start.12) | collective-permute-done | bytes 98336 | tf_op jit(solution)/shard_map/ppermute | solution.py:259
  58.0 3.5 %collective-permute-done.13.r2 = bf16[384,128]{1,0:T(8,128)(2,1)S(1)} collective-permute-done((bf16[384,128]{1,0:T(8,128)(2,1)S(1)}, bf16[384,128]{1,0:T(8,128)(2,1)S(1)}, u32[]{:S(2)}, u32[]{:S(2)}) %collective-permute-start.13) | collective-permute-done | bytes 98336 | tf_op jit(solution)/shard_map/ppermute | solution.py:259
  61.5 1.6 %collective-permute-done.14.r3 = bf16[384,128]{1,0:T(8,128)(2,1)S(1)} collective-permute-done((bf16[384,128]{1,0:T(8,128)(2,1)S(1)}, bf16[384,128]{1,0:T(8,128)(2,1)S(1)}, u32[]{:S(2)}, u32[]{:S(2)}) %collective-permute-start.14) | collective-permute-done | bytes 98336 | tf_op jit(solution)/shard_map/ppermute | solution.py:259
  63.1 0.7 %shard_map.91 = (bf16[256,128]{1,0:T(8,128)(2,1)}, f32[128,128]{1,0:T(8,128)}) custom-call(f32[256,128]{1,0:T(8,128)S(1)} %get-tuple-element.29.keep_z, bf16[128,128]{1,0:T(8,128)(2,1)S(1)} %get-tuple-element.30.keep_zw, bf16[384,128]{1,0:T(8,128)(2,1)S(1)} %collective-permute-done.12.r1, bf16[384,128]{1,0:T(8,128)(2,1)S(1)} %collective-permute-done.13.r2, ...), custom_call_target="tpu_custom_call" | custom-call | tf_op jit(solution)/shard_map/pallas_call | solution.py:264
  (6 shorter events, 0.2 us)
Async XLA Ops:
  1.8 4.3 %collective-permute-start = (bf16[256,256]{1,0:T(8,128)(2,1)S(1)}, bf16[256,256]{1,0:T(8,128)(2,1)S(1)}, u32[]{:S(2)}, u32[]{:S(2)}) collective-permute-start(bf16[256,256]{1,0:T(8,128)(2,1)S(1)} %shard_map.87.own), channel_id=1, source_target_pairs={{0,1},{1,0},{2,3},{3,2},{4,5},{5,4},{6,7},{7,6},{8,9},{9,8},{10,11... | collective-permute-start | bytes 393224 | tf_op jit(solution)/shard_map/ppermute | solution.py:222
  6.7 10.3 %collective-permute-start.4 = (bf16[320,256]{1,0:T(8,128)(2,1)S(1)}, bf16[320,256]{1,0:T(8,128)(2,1)S(1)}, u32[]{:S(2)}, u32[]{:S(2)}) collective-permute-start(bf16[320,256]{1,0:T(8,128)(2,1)S(1)} %shard_map.88.refs_0_), channel_id=1, source_target_pairs={{0,6},{1,15},{2,0},{3,9},{4,2},{5,11},{6,4},{7,13},{8,14},{9,7},{1... | collective-permute-start | bytes 491528 | tf_op jit(solution)/shard_map/ppermute | solution.py:236
  8.9 8.2 %collective-permute-start.3 = (bf16[320,256]{1,0:T(8,128)(2,1)S(1)}, bf16[320,256]{1,0:T(8,128)(2,1)S(1)}, u32[]{:S(2)}, u32[]{:S(2)}) collective-permute-start(bf16[320,256]{1,0:T(8,128)(2,1)S(1)} %shard_map.88.refs_0_), channel_id=1, source_target_pairs={{0,4},{1,13},{2,6},{3,15},{4,0},{5,9},{6,2},{7,11},{8,12},{9,5},{1... | collective-permute-start | bytes 491528 | tf_op jit(solution)/shard_map/ppermute | solution.py:236
  9.2 8.2 %collective-permute-start.2 = (bf16[320,256]{1,0:T(8,128)(2,1)S(1)}, bf16[320,256]{1,0:T(8,128)(2,1)S(1)}, u32[]{:S(2)}, u32[]{:S(2)}) collective-permute-start(bf16[320,256]{1,0:T(8,128)(2,1)S(1)} %shard_map.88.refs_0_), channel_id=1, source_target_pairs={{0,2},{1,11},{2,4},{3,13},{4,6},{5,15},{6,0},{7,9},{8,10},{9,3},{1... | collective-permute-start | bytes 491528 | tf_op jit(solution)/shard_map/ppermute | solution.py:236
  10.9 6.5 %collective-permute-start.1 = (bf16[320,256]{1,0:T(8,128)(2,1)S(1)}, bf16[320,256]{1,0:T(8,128)(2,1)S(1)}, u32[]{:S(2)}, u32[]{:S(2)}) collective-permute-start(bf16[320,256]{1,0:T(8,128)(2,1)S(1)} %shard_map.88.refs_0_), channel_id=1, source_target_pairs={{1,9},{3,11},{5,13},{7,15},{9,1},{11,3},{13,5},{15,7},{17,25},{19,... | collective-permute-start | bytes 491528 | tf_op jit(solution)/shard_map/ppermute | solution.py:236
  17.4 3.9 %collective-permute-start.5 = (bf16[320,256]{1,0:T(8,128)(2,1)S(1)}, bf16[320,256]{1,0:T(8,128)(2,1)S(1)}, u32[]{:S(2)}, u32[]{:S(2)}) collective-permute-start(bf16[320,256]{1,0:T(8,128)(2,1)S(1)} %collective-permute-done.1.refs_1_), channel_id=1, source_target_pairs={{0,1},{1,0},{2,3},{3,2},{4,5},{5,4},{6,7},{7,6},{8,9},{9,8},{10,11... | collective-permute-start | bytes 491528 | tf_op jit(solution)/shard_map/ppermute | solution.py:240
  20.2 1.4 %collective-permute-start.6 = (bf16[320,256]{1,0:T(8,128)(2,1)S(1)}, bf16[320,256]{1,0:T(8,128)(2,1)S(1)}, u32[]{:S(2)}, u32[]{:S(2)}) collective-permute-start(bf16[320,256]{1,0:T(8,128)(2,1)S(1)} %collective-permute-done.2.refs_2_), channel_id=1, source_target_pairs={{0,1},{1,0},{2,3},{3,2},{4,5},{5,4},{6,7},{7,6},{8,9},{9,8},{10,11... | collective-permute-start | bytes 491528 | tf_op jit(solution)/shard_map/ppermute | solution.py:240
  20.2 1.6 %collective-permute-start.7 = (bf16[320,256]{1,0:T(8,128)(2,1)S(1)}, bf16[320,256]{1,0:T(8,128)(2,1)S(1)}, u32[]{:S(2)}, u32[]{:S(2)}) collective-permute-start(bf16[320,256]{1,0:T(8,128)(2,1)S(1)} %collective-permute-done.3.refs_3_), channel_id=1, source_target_pairs={{0,1},{1,0},{2,3},{3,2},{4,5},{5,4},{6,7},{7,6},{8,9},{9,8},{10,11... | collective-permute-start | bytes 491528 | tf_op jit(solution)/shard_map/ppermute | solution.py:240
  20.7 1.4 %collective-permute-start.8 = (bf16[320,256]{1,0:T(8,128)(2,1)S(1)}, bf16[320,256]{1,0:T(8,128)(2,1)S(1)}, u32[]{:S(2)}, u32[]{:S(2)}) collective-permute-start(bf16[320,256]{1,0:T(8,128)(2,1)S(1)} %collective-permute-done.4.refs_4_), channel_id=1, source_target_pairs={{0,1},{1,0},{2,3},{3,2},{4,5},{5,4},{6,7},{7,6},{8,9},{9,8},{10,11... | collective-permute-start | bytes 491528 | tf_op jit(solution)/shard_map/ppermute | solution.py:240
  29.5 9.1 %collective-permute-start.9 = (bf16[1152,128]{1,0:T(8,128)(2,1)S(1)}, bf16[1152,128]{1,0:T(8,128)(2,1)S(1)}, u32[]{:S(2)}, u32[]{:S(2)}) collective-permute-start(bf16[1152,128]{1,0:T(8,128)(2,1)S(1)} %get-tuple-element.26), channel_id=1, source_target_pairs={{0,16},{16,32},{32,48},{48,0},{1,17},{17,33},{33,49},{49,1},{2,18}... | collective-permute-start | bytes 884744 | tf_op jit(solution)/shard_map/ppermute | solution.py:253
  29.6 13.9 %collective-permute-start.10 = (bf16[1152,128]{1,0:T(8,128)(2,1)S(1)}, bf16[1152,128]{1,0:T(8,128)(2,1)S(1)}, u32[]{:S(2)}, u32[]{:S(2)}) collective-permute-start(bf16[1152,128]{1,0:T(8,128)(2,1)S(1)} %get-tuple-element.27), channel_id=1, source_target_pairs={{0,32},{16,48},{32,0},{48,16},{1,33},{17,49},{33,1},{49,17},{2,34}... | collective-permute-start | bytes 884744 | tf_op jit(solution)/shard_map/ppermute | solution.py:253
  30.8 14.3 %collective-permute-start.11 = (bf16[1152,128]{1,0:T(8,128)(2,1)S(1)}, bf16[1152,128]{1,0:T(8,128)(2,1)S(1)}, u32[]{:S(2)}, u32[]{:S(2)}) collective-permute-start(bf16[1152,128]{1,0:T(8,128)(2,1)S(1)} %get-tuple-element.28), channel_id=1, source_target_pairs={{0,48},{16,0},{32,16},{48,32},{1,49},{17,1},{33,17},{49,33},{2,50}... | collective-permute-start | bytes 884744 | tf_op jit(solution)/shard_map/ppermute | solution.py:253
  45.7 12.3 %collective-permute-start.12 = (bf16[384,128]{1,0:T(8,128)(2,1)S(1)}, bf16[384,128]{1,0:T(8,128)(2,1)S(1)}, u32[]{:S(2)}, u32[]{:S(2)}) collective-permute-start(bf16[384,128]{1,0:T(8,128)(2,1)S(1)} %get-tuple-element.31), channel_id=1, source_target_pairs={{0,64},{64,128},{128,192},{192,0},{1,65},{65,129},{129,193},{193,1... | collective-permute-start | bytes 294920 | tf_op jit(solution)/shard_map/ppermute | solution.py:259
  45.8 15.7 %collective-permute-start.13 = (bf16[384,128]{1,0:T(8,128)(2,1)S(1)}, bf16[384,128]{1,0:T(8,128)(2,1)S(1)}, u32[]{:S(2)}, u32[]{:S(2)}) collective-permute-start(bf16[384,128]{1,0:T(8,128)(2,1)S(1)} %get-tuple-element.32), channel_id=1, source_target_pairs={{0,128},{64,192},{128,0},{192,64},{1,129},{65,193},{129,1},{193,65... | collective-permute-start | bytes 294920 | tf_op jit(solution)/shard_map/ppermute | solution.py:259
  54.5 8.6 %collective-permute-start.14 = (bf16[384,128]{1,0:T(8,128)(2,1)S(1)}, bf16[384,128]{1,0:T(8,128)(2,1)S(1)}, u32[]{:S(2)}, u32[]{:S(2)}) collective-permute-start(bf16[384,128]{1,0:T(8,128)(2,1)S(1)} %get-tuple-element.33), channel_id=1, source_target_pairs={{0,192},{64,0},{128,64},{192,128},{1,193},{65,1},{129,65},{193,129... | collective-permute-start | bytes 294920 | tf_op jit(solution)/shard_map/ppermute | solution.py:259

commit v3 on v2

v3 whole, which is shorter than its diff:
```python
import functools
import itertools

import jax
import jax.numpy as jnp
from jax import lax
from jax.experimental import pallas as pl
from jax.experimental.pallas import tpu as pltpu
from jax.sharding import Mesh, PartitionSpec as P

bf16 = jnp.bfloat16
f32 = jnp.float32
i32 = jnp.int32
T = 128
ROWS = ("zh", "y")
COLS = ("zl", "x", "core")
BLOCKS = 32
SLOTS = 256
PLACES = 384
PART = 32
UNROLL = 32
NOWHERE = 31
LIMIT = 16 * 1024 * 1024


def spec(space=pltpu.VMEM):
    return pl.BlockSpec(memory_space=space)


def split_parts(value):
    high = value.astype(bf16)
    low = (value - high.astype(f32)).astype(bf16)
    return high, low


def ring_sum(own, received):
    return (own + received[1]) + (received[0] + received[2])


def local_kernel(inputs, message):
    n = (inputs.shape[0] - T) // 3
    og, pre, agg = (inputs[pl.ds(i * n, n), :] for i in range(3))
    weight = inputs[3 * n :, :]
    grad_pre = jnp.where(pre > 0, og, jnp.zeros_like(og))
    message[0:T, :] = lax.dot_general(
        weight, grad_pre, (((1,), (1,)), ((), ())), preferred_element_type=f32
    ).astype(bf16)
    partial = lax.dot_general(
        agg, grad_pre, (((0,), (0,)), ((), ())), preferred_element_type=f32
    )
    high, low = split_parts(partial)
    message[T : 2 * T, 0:T] = high
    message[T : 2 * T, T : 2 * T] = low


def chip_kernel(pos, own, other, message):
    core = pos[4]
    message[pl.ds(pl.multiple_of(core * T, T), T), :] = own[0:T, :]
    message[pl.ds(pl.multiple_of((1 - core) * T, T), T), :] = other[0:T, :]
    sums = [m[T : 2 * T, 0:T].astype(f32) + m[T : 2 * T, T : 2 * T].astype(f32) for m in (own, other)]
    total = (sums[0] + sums[1]).astype(bf16)
    message[2 * T : 2 * T + 64, 0:T] = total[0:64, :]
    message[2 * T : 2 * T + 64, T : 2 * T] = total[64:T, :]


def order_kernel(pos, count_ref, coords_hbm, tiles_hbm, out, tiles, coords, listed, sems):
    fetches = [
        pltpu.make_async_copy(tiles_hbm.at[part], tiles.at[part], sems.at[1 + i])
        for i, part in enumerate(pl.ds(g * PART, PART) for g in range(SLOTS // PART))
    ]
    fetch_coords = pltpu.make_async_copy(coords_hbm, coords, sems.at[0])
    fetch_coords.start()
    for fetch in fetches:
        fetch.start()
    fetch_coords.wait()
    count, y = count_ref[0], pos[1]
    shape = (SLOTS, SLOTS)
    at_k = lax.broadcasted_iota(i32, shape, 0)
    at_j = lax.broadcasted_iota(i32, shape, 1)
    live_j = at_j < count

    def down(value_j):
        return jnp.sum(jnp.where(at_k == at_j, value_j, 0), axis=1, keepdims=True)

    col_j = coords[1:2, :]
    offset_j = (((col_j >> 1) & 3) - y) & 3
    stage_j = jnp.where(offset_j == 2, 0, jnp.where(offset_j == 0, 2, 1))
    local_j = (col_j >> 3) * 2 + (col_j & 1) + jnp.where(offset_j == 3, 8, 0)
    slot_j = lax.broadcasted_iota(i32, (1, SLOTS), 1)
    code_k = down(slot_j + (coords[0:1, :] << 8) + (local_j << 16))
    stage_k = down(stage_j)
    before = live_j & (stage_j == stage_k) & (at_j < at_k)
    place_k = jnp.sum(before.astype(i32), axis=1, keepdims=True)
    lane = lax.broadcasted_iota(i32, (1, PLACES), 1)
    base = jnp.zeros((1, 1), i32)
    numbers = jnp.zeros((1, PLACES), i32)
    for stage in range(3):
        place_k += jnp.where(stage_k == stage, base, 0)
        members = ((slot_j < count) & (stage_j == stage)).astype(i32)
        groups = (jnp.sum(members, axis=1, keepdims=True) + UNROLL - 1) // UNROLL
        numbers = jnp.where(lane == PLACES - 3 + stage, groups, numbers)
        base += groups * UNROLL
    slot_k = lax.broadcasted_iota(i32, (SLOTS, 1), 0)
    place_k = jnp.where(slot_k < count, place_k, -1)
    hit = lax.broadcasted_iota(i32, (SLOTS, PLACES), 1) == place_k
    code = jnp.sum(jnp.where(hit, code_k + 1, 0), axis=0, keepdims=True) - 1
    code = jnp.where(code < 0, NOWHERE << 16, code)
    listed[...] = jnp.where(lane >= PLACES - 3, numbers, code)
    hand_over = pltpu.make_async_copy(listed, out, sems.at[0])
    hand_over.start()
    hand_over.wait()
    for fetch in fetches:
        fetch.wait()


def multiply(stage, order, grads, tiles, acc):
    acc[...] = jnp.zeros_like(acc)
    spare = acc.shape[0] - 1
    groups = [order[0, PLACES - 3 + i] for i in range(3)]
    base = sum(groups[:stage], 0)

    @pl.loop(0, groups[stage])
    def _(group):
        for u in range(UNROLL):
            code = order[0, (base + group) * UNROLL + u]
            at = jnp.minimum(code >> 16, spare)
            acc[at] += jnp.dot(
                grads[(code >> 8) & 31], tiles[code & 255], preferred_element_type=f32
            )


def first_kernel(pos, order, *refs):
    mine, got, swapped = refs[0], refs[1:5], refs[5:9]
    tiles, grads, weight_part, send, acc, parts = refs[9:]
    zl, x, core = pos[2], pos[3], pos[4]

    arrived = [(got[k], core, k) for k in range(4)]
    arrived += [(swapped[k], 1 - core, k) for k in range(4)]
    arrived += [(mine, 0, 0)]
    for message, dz, dx in arrived:
        chip = ((zl + 2 - dz) % 2) * 4 + (x + 4 - dx) % 4
        for c in range(2):
            for h in range(2):
                grads[chip * 4 + 2 * c + h] = message[c * T : (c + 1) * T, h * T : (h + 1) * T]
        parts[chip] = message[2 * T : 2 * T + 64, :]
    total = parts[0].astype(f32)
    for chip in range(1, 8):
        total += parts[chip].astype(f32)
    rounded = total.astype(bf16)
    weight_part[0:64, :] = rounded[:, 0:T]
    weight_part[64:T, :] = rounded[:, T : 2 * T]
    multiply(0, order, grads, tiles, acc)
    for i in range(8):
        send[i * T : (i + 1) * T, :] = acc[i].astype(bf16)


def second_kernel(order, grads, tiles, send_1, send_3, acc):
    multiply(1, order, grads, tiles, acc)
    for i in range(8):
        send_1[i * T : (i + 1) * T, :] = acc[i].astype(bf16)
        send_3[i * T : (i + 1) * T, :] = acc[8 + i].astype(bf16)


def third_kernel(order, grads, tiles, keep, acc):
    multiply(2, order, grads, tiles, acc)
    for i in range(8):
        keep[i * T : (i + 1) * T, :] = acc[i]


def y_kernel(pos, keep, r1, r2, r3, keep_z, s1, s2, s3):
    zh_me = pos[0]
    for d, out in enumerate((keep_z, s1, s2, s3)):
        rows = pl.ds(pl.multiple_of(((zh_me + d) % 4) * 256, 256), 256)
        total = keep[rows, :]
        for r in (r1, r2, r3):
            total += r[rows, :].astype(f32)
        out[...] = total.astype(out.dtype)


def weight_kernel(own, r1, r2, r3, out):
    parts = [r[...].astype(f32) for r in (r1, r2, r3)]
    out[...] = ring_sum(own[...].astype(f32), parts).astype(bf16)


def z_kernel(scale, keep_z, r1, r2, r3, w0, w1, w2, w3, out, weight_out):
    parts = [w[...].astype(f32) for w in (w1, w2, w3)]
    weight_out[...] = ring_sum(w0[...].astype(f32), parts) * scale
    for h in range(2):
        rows = pl.ds(h * T, T)
        total = keep_z[rows, :]
        for r in (r1, r2, r3):
            total += r[rows, :].astype(f32)
        out[rows, :] = total.T.astype(bf16)


def call(kernel, out_shape, in_specs, scratch=(), cost=None, out_specs=None):
    return pl.pallas_call(
        kernel,
        out_shape=out_shape,
        in_specs=in_specs,
        out_specs=out_specs or jax.tree.map(lambda _: spec(), out_shape),
        scratch_shapes=list(scratch),
        compiler_params=pltpu.CompilerParams(vmem_limit_bytes=LIMIT),
        cost_estimate=cost,
    )


def struct(*shape, dtype=bf16):
    return jax.ShapeDtypeStruct(shape, dtype)


def chip_perm(k):
    pairs = []
    for z, x, c in itertools.product(range(2), range(4), range(2)):
        if c or k:
            pairs.append(((z * 4 + x) * 2 + c, (((z + c) % 2) * 4 + (x + k) % 4) * 2 + c))
    return pairs


def body(out_grad, preact, aggregated, weight, tiles, tile_coords, tile_count):
    smem, vmem, hbm = spec(pltpu.SMEM), spec(), spec(pltpu.HBM)
    nodes = out_grad.shape[0]
    pos = jnp.stack([lax.axis_index(a) for a in ROWS + COLS]).astype(i32)
    swap = [(0, 1), (1, 0)]
    inputs = jnp.concatenate([out_grad, preact, aggregated, weight], 0)
    local = call(local_kernel, struct(2 * T, nodes), [vmem])(inputs)
    mine = call(chip_kernel, struct(2 * T + 64, nodes), [smem, vmem, vmem])(
        pos, local, lax.ppermute(local, "core", swap)
    )
    order, held = call(
        order_kernel,
        [pltpu.SMEM((1, PLACES), i32), pltpu.VMEM((SLOTS, T, T), bf16)],
        [smem, smem, hbm, hbm],
        [pltpu.VMEM((2, SLOTS), i32), pltpu.VMEM((1, PLACES), i32), pltpu.SemaphoreType.DMA((1 + SLOTS // PART,))],
        pl.CostEstimate(flops=0, bytes_accessed=2 * SLOTS * T * T * 2, transcendentals=0),
        (smem, vmem),
    )(
        pos,
        tile_count.reshape(1),
        pltpu.with_memory_space_constraint(tile_coords.reshape(2, SLOTS), pltpu.HBM),
        pltpu.with_memory_space_constraint(tiles.reshape(SLOTS, T, T), pltpu.HBM),
    )
    got = [lax.ppermute(mine, COLS, chip_perm(k)) for k in range(4)]
    swapped = []
    for k in range(4):
        ready = got[k]
        if k == 3:
            ready, _ = lax.optimization_barrier((ready, order))
        swapped.append(lax.ppermute(ready, "core", swap))
    cost = lambda share: pl.CostEstimate(
        flops=share * SLOTS * 2 * T**3, bytes_accessed=share * SLOTS * T * T * 2, transcendentals=0
    )
    grads, weight_part, send_2 = call(
        first_kernel,
        [struct(BLOCKS, T, T), struct(T, T), struct(8 * T, T)],
        [smem] * 2 + [vmem] * 10,
        [pltpu.VMEM((9, T, T), f32), pltpu.VMEM((8, 64, 2 * T), bf16)],
        cost(1),
    )(pos, order, mine, *got, *swapped, held)
    send_1, send_3 = call(
        second_kernel,
        [struct(8 * T, T)] * 2,
        [smem] + [vmem] * 2,
        [pltpu.VMEM((17, T, T), f32)],
        cost(1),
    )(order, grads, held)
    keep = call(
        third_kernel,
        struct(8 * T, T, dtype=f32),
        [smem] + [vmem] * 2,
        [pltpu.VMEM((9, T, T), f32)],
        cost(1),
    )(order, grads, held)
    turn = lambda d: [(i, (i + d) % 4) for i in range(4)]
    around = lambda axis, values: [lax.ppermute(v, axis, turn(d)) for d, v in zip((1, 2, 3), values)]
    got = around("y", (send_1, send_2, send_3))
    weight_zs = around("zh", [weight_part] * 3)
    keep_z, *sends = call(
        y_kernel,
        [struct(256, T, dtype=f32)] + [struct(256, T)] * 3,
        [smem] + [vmem] * 4,
    )(pos, keep, *got)
    weight_z = call(weight_kernel, struct(T, T), [vmem] * 4)(weight_part, *weight_zs)
    weight_ys = around("y", [weight_z] * 3)
    got = around("zh", sends)
    devices = 1
    for a in ROWS + COLS:
        devices *= lax.axis_size(a)
    scale = 1.0 / (nodes * devices) ** 0.5
    input_grad, weight_grad = call(
        functools.partial(z_kernel, scale),
        [struct(nodes, T), struct(T, T, dtype=f32)],
        [vmem] * 8,
    )(keep_z, *got, weight_z, *weight_ys)
    return input_grad, weight_grad


def solution(mesh):
    fine = Mesh(mesh.devices.reshape(4, 4, 2, 4, 2), ROWS + COLS)
    every = ROWS + COLS
    return jax.shard_map(
        body,
        mesh=fine,
        in_specs=(
            P(every, None),
            P(every, None),
            P(every, None),
            P(),
            P(ROWS, COLS, None, None, None),
            P(ROWS, COLS, None, None),
            P(ROWS, COLS),
        ),
        out_specs=(P(every, None), P()),
        check_vma=False,
    )
```

time: 63.4 us -> 61 us (0.962)
  the two profiles are of different devices: /device:TPU:1 before, /device:TPU:32 now
where the time goes in v3:
time: 61 us; the launch traced here: 61.1 us
  starting transfers between devices  31.3 us (51%)
  waiting for transfers between devices  17.2 us (28%)
  Pallas kernels  10.2 us (17%)
  between operations  1.39 us (2%)
  other arithmetic  0.94 us (2%)
    ppermute x12, starting transfers between devices, body(): lax.ppermute(v, axis, turn(d))  25.5 us
    ppermute x12, waiting for transfers between devices, body(): lax.ppermute(v, axis, turn(d))  10.1 us
    ppermute x4, starting transfers between devices, body(): got = [lax.ppermute(mine, COLS, chip_perm(k)) for k in range(4)]  5.18 us
    ppermute x4, waiting for transfers between devices, body(): got = [lax.ppermute(mine, COLS, chip_perm(k)) for k in range(4)]  4.39 us
    pallas_call x1, Pallas kernels, body(): call(order_kernel, [pltpu.SMEM((1, PLACES), i32), pltpu.VMEM((SLOTS, T, T...  4.04 us
    pallas_call x1, Pallas kernels, body(): call(second_kernel, [struct(8 * T, T)] * 2, [smem] + [vmem] * 2, [pltpu.V...  1.57 us
    ppermute x4, waiting for transfers between devices, body(): swapped.append(lax.ppermute(ready, 'core', swap))  1.39 us
    pallas_call x1, Pallas kernels, body(): call(first_kernel, [struct(BLOCKS, T, T), struct(T, T), struct(8 * T, T)]...  1.33 us
  transfers between devices with their start and end apart: 21, of which 12 were waited for; matrix products, arithmetic and copies ran while one was open for 0% of the time, Pallas kernels for 12%

profile of v3, /device:TPU:32, one launch (start us, length us, event | category | flops | bytes accessed | tf_op | source)
XLA Modules:
  0.0 61.1 jit_solution(7931085281210757737)
XLA Ops:
  0.6 0.9 %pad_maximum_fusion.inputs = bf16[896,128]{1,0:T(8,128)(2,1)S(1)} fusion(bf16[128,128]{1,0:T(8,128)(2,1)} %param.10, bf16[256,128]{1,0:T(8,128)(2,1)} %param.9, bf16[256,128]{1,0:T(8,128)(2,1)} %param.8, bf16[256,128]{1,0:T(8,128)(2,1)} %param.7), kind=kLoop, calls=%fused_computation | loop fusion | flops 917504 | bytes 458752 | tf_op jit(solution)/shard_map/concatenate | solution.py:225
  2.0 1.2 %collective-permute-done.other = bf16[256,256]{1,0:T(8,128)(2,1)S(1)} collective-permute-done((bf16[256,256]{1,0:T(8,128)(2,1)S(1)}, bf16[256,256]{1,0:T(8,128)(2,1)S(1)}, u32[]{:S(2)}, u32[]{:S(2)}) %collective-permute-start) | collective-permute-done | bytes 131104 | tf_op jit(solution)/shard_map/ppermute | solution.py:228
  3.2 0.6 shard_map.88.refs_0_
  3.8 2.8 %collective-permute-start.4 = (bf16[320,256]{1,0:T(8,128)(2,1)S(1)}, bf16[320,256]{1,0:T(8,128)(2,1)S(1)}, u32[]{:S(2)}, u32[]{:S(2)}) collective-permute-start(bf16[320,256]{1,0:T(8,128)(2,1)S(1)} %shard_map.88.refs_0_), channel_id=1, source_target_pairs={{0,6},{1,15},{2,0},{3,9},{4,2},{5,11},{6,4},{7,13},{8,14},{9,7},{1... | collective-permute-start | bytes 491528 | tf_op jit(solution)/shard_map/ppermute | solution.py:243
  6.6 0.8 %collective-permute-start.3 = (bf16[320,256]{1,0:T(8,128)(2,1)S(1)}, bf16[320,256]{1,0:T(8,128)(2,1)S(1)}, u32[]{:S(2)}, u32[]{:S(2)}) collective-permute-start(bf16[320,256]{1,0:T(8,128)(2,1)S(1)} %shard_map.88.refs_0_), channel_id=1, source_target_pairs={{0,4},{1,13},{2,6},{3,15},{4,0},{5,9},{6,2},{7,11},{8,12},{9,5},{1... | collective-permute-start | bytes 491528 | tf_op jit(solution)/shard_map/ppermute | solution.py:243
  7.4 0.9 %collective-permute-start.2 = (bf16[320,256]{1,0:T(8,128)(2,1)S(1)}, bf16[320,256]{1,0:T(8,128)(2,1)S(1)}, u32[]{:S(2)}, u32[]{:S(2)}) collective-permute-start(bf16[320,256]{1,0:T(8,128)(2,1)S(1)} %shard_map.88.refs_0_), channel_id=1, source_target_pairs={{0,2},{1,11},{2,4},{3,13},{4,6},{5,15},{6,0},{7,9},{8,10},{9,3},{1... | collective-permute-start | bytes 491528 | tf_op jit(solution)/shard_map/ppermute | solution.py:243
  8.3 0.7 %collective-permute-start.1 = (bf16[320,256]{1,0:T(8,128)(2,1)S(1)}, bf16[320,256]{1,0:T(8,128)(2,1)S(1)}, u32[]{:S(2)}, u32[]{:S(2)}) collective-permute-start(bf16[320,256]{1,0:T(8,128)(2,1)S(1)} %shard_map.88.refs_0_), channel_id=1, source_target_pairs={{1,9},{3,11},{5,13},{7,15},{9,1},{11,3},{13,5},{15,7},{17,25},{19,... | collective-permute-start | bytes 491528 | tf_op jit(solution)/shard_map/ppermute | solution.py:243
  9.6 4.0 %shard_map.86 = (s32[1,384]{1,0:T(1,128)S(4)}, bf16[256,128,128]{2,1,0:T(8,128)(2,1)S(1)}) custom-call(s32[5]{0:T(128)S(1)} %stack.23.pos, s32[1]{0:T(128)} %bitcast.8.count_ref, s32[2,256]{1,0:T(2,128)} %bitcast.10, bf16[256,128,128]{2,1,0:T(8,128)(2,1)} %bitcast.9), custom_call_target="tpu_custom_call" | custom-call | bytes 16777216 | tf_op jit(solution)/shard_map/pallas_call | solution.py:230
  13.7 1.1 %collective-permute-done.4.refs_4_ = bf16[320,256]{1,0:T(8,128)(2,1)S(1)} collective-permute-done((bf16[320,256]{1,0:T(8,128)(2,1)S(1)}, bf16[320,256]{1,0:T(8,128)(2,1)S(1)}, u32[]{:S(2)}, u32[]{:S(2)}) %collective-permute-start.4) | collective-permute-done | bytes 163872 | tf_op jit(solution)/shard_map/ppermute | solution.py:243
  14.7 1.7 %collective-permute-done.3.refs_3_ = bf16[320,256]{1,0:T(8,128)(2,1)S(1)} collective-permute-done((bf16[320,256]{1,0:T(8,128)(2,1)S(1)}, bf16[320,256]{1,0:T(8,128)(2,1)S(1)}, u32[]{:S(2)}, u32[]{:S(2)}) %collective-permute-start.3) | collective-permute-done | bytes 163872 | tf_op jit(solution)/shard_map/ppermute | solution.py:243
  16.4 1.6 %collective-permute-done.2.refs_2_ = bf16[320,256]{1,0:T(8,128)(2,1)S(1)} collective-permute-done((bf16[320,256]{1,0:T(8,128)(2,1)S(1)}, bf16[320,256]{1,0:T(8,128)(2,1)S(1)}, u32[]{:S(2)}, u32[]{:S(2)}) %collective-permute-start.2) | collective-permute-done | bytes 163872 | tf_op jit(solution)/shard_map/ppermute | solution.py:243
  18.1 0.5 collective-permute-start.5
  18.6 0.9 %collective-permute-done.6.refs_6_ = bf16[320,256]{1,0:T(8,128)(2,1)S(1)} collective-permute-done((bf16[320,256]{1,0:T(8,128)(2,1)S(1)}, bf16[320,256]{1,0:T(8,128)(2,1)S(1)}, u32[]{:S(2)}, u32[]{:S(2)}) %collective-permute-start.6) | collective-permute-done | bytes 163872 | tf_op jit(solution)/shard_map/ppermute | solution.py:249
  20.0 1.3 %shard_map.89 = (bf16[32,128,128]{2,1,0:T(8,128)(2,1)S(1)}, bf16[128,128]{1,0:T(8,128)(2,1)S(1)}, bf16[1024,128]{1,0:T(8,128)(2,1)S(1)}) custom-call(s32[5]{0:T(128)S(1)} %stack.23.pos, s32[1,384]{1,0:T(1,128)S(4)} %get-tuple-element.14.order, bf16[320,256]{1,0:T(8,128)(2,1)S(1)} %shard_map.88.refs_0_, bf16[320,256]{1,0:T(8,128)(2,1)S(1)} %collective-permute-done.1.refs_1_, ...), custom_call_target="tpu_custom_call" | custom-call | flops 1073741824 | bytes 8388608 | tf_op jit(solution)/shard_map/pallas_call | solution.py:253
  21.3 3.3 %collective-permute-start.10 = (bf16[1024,128]{1,0:T(8,128)(2,1)S(1)}, bf16[1024,128]{1,0:T(8,128)(2,1)S(1)}, u32[]{:S(2)}, u32[]{:S(2)}) collective-permute-start(bf16[1024,128]{1,0:T(8,128)(2,1)S(1)} %get-tuple-element.19), channel_id=1, source_target_pairs={{0,32},{16,48},{32,0},{48,16},{1,33},{17,49},{33,1},{49,17},{2,34}... | collective-permute-start | bytes 786440 | tf_op jit(solution)/shard_map/ppermute | solution.py:275
  24.6 1.6 %shard_map.91 = (bf16[1024,128]{1,0:T(8,128)(2,1)S(1)}, bf16[1024,128]{1,0:T(8,128)(2,1)S(1)}) custom-call(s32[1,384]{1,0:T(1,128)S(4)} %get-tuple-element.14.order, bf16[32,128,128]{2,1,0:T(8,128)(2,1)S(1)} %get-tuple-element.17.grads, bf16[256,128,128]{2,1,0:T(8,128)(2,1)S(1)} %get-tuple-element.16.refs_9_.tiles), custom_call_target="tpu_custom_call" | custom-call | flops 1073741824 | bytes 8388608 | tf_op jit(solution)/shard_map/pallas_call | solution.py:260
  26.5 3.0 %collective-permute-start.11 = (bf16[1024,128]{1,0:T(8,128)(2,1)S(1)}, bf16[1024,128]{1,0:T(8,128)(2,1)S(1)}, u32[]{:S(2)}, u32[]{:S(2)}) collective-permute-start(bf16[1024,128]{1,0:T(8,128)(2,1)S(1)} %get-tuple-element.20), channel_id=1, source_target_pairs={{0,48},{16,0},{32,16},{48,32},{1,49},{17,1},{33,17},{49,33},{2,50}... | collective-permute-start | bytes 786440 | tf_op jit(solution)/shard_map/ppermute | solution.py:275
  29.5 6.1 %collective-permute-start.17 = (bf16[128,128]{1,0:T(8,128)(2,1)S(1)}, bf16[128,128]{1,0:T(8,128)(2,1)S(1)}, u32[]{:S(2)}, u32[]{:S(2)}) collective-permute-start(bf16[128,128]{1,0:T(8,128)(2,1)S(1)} %get-tuple-element.25.own), channel_id=1, source_target_pairs={{0,192},{64,0},{128,64},{192,128},{1,193},{65,1},{129,65},{193,129... | collective-permute-start | bytes 98312 | tf_op jit(solution)/shard_map/ppermute | solution.py:275
  35.6 0.8 %collective-permute-start.16 = (bf16[128,128]{1,0:T(8,128)(2,1)S(1)}, bf16[128,128]{1,0:T(8,128)(2,1)S(1)}, u32[]{:S(2)}, u32[]{:S(2)}) collective-permute-start(bf16[128,128]{1,0:T(8,128)(2,1)S(1)} %get-tuple-element.25.own), channel_id=1, source_target_pairs={{0,128},{64,192},{128,0},{192,64},{1,129},{65,193},{129,1},{193,65... | collective-permute-start | bytes 98312 | tf_op jit(solution)/shard_map/ppermute | solution.py:275
  36.3 0.8 %collective-permute-done.17.r3 = bf16[128,128]{1,0:T(8,128)(2,1)S(1)} collective-permute-done((bf16[128,128]{1,0:T(8,128)(2,1)S(1)}, bf16[128,128]{1,0:T(8,128)(2,1)S(1)}, u32[]{:S(2)}, u32[]{:S(2)}) %collective-permute-start.17) | collective-permute-done | bytes 32800 | tf_op jit(solution)/shard_map/ppermute | solution.py:275
  37.2 1.7 %collective-permute-start.15 = (bf16[128,128]{1,0:T(8,128)(2,1)S(1)}, bf16[128,128]{1,0:T(8,128)(2,1)S(1)}, u32[]{:S(2)}, u32[]{:S(2)}) collective-permute-start(bf16[128,128]{1,0:T(8,128)(2,1)S(1)} %get-tuple-element.25.own), channel_id=1, source_target_pairs={{0,64},{64,128},{128,192},{192,0},{1,65},{65,129},{129,193},{193,1... | collective-permute-start | bytes 98312 | tf_op jit(solution)/shard_map/ppermute | solution.py:275
  38.8 1.0 %shard_map.90.keep = f32[1024,128]{1,0:T(8,128)S(1)} custom-call(s32[1,384]{1,0:T(1,128)S(4)} %get-tuple-element.14.order, bf16[32,128,128]{2,1,0:T(8,128)(2,1)S(1)} %get-tuple-element.17.grads, bf16[256,128,128]{2,1,0:T(8,128)(2,1)S(1)} %get-tuple-element.16.refs_9_.tiles), custom_call_target="tpu_custom_call" | custom-call | flops 1073741824 | bytes 8388608 | tf_op jit(solution)/shard_map/pallas_call | solution.py:267
  39.9 3.5 %collective-permute-done.16.r2 = bf16[128,128]{1,0:T(8,128)(2,1)S(1)} collective-permute-done((bf16[128,128]{1,0:T(8,128)(2,1)S(1)}, bf16[128,128]{1,0:T(8,128)(2,1)S(1)}, u32[]{:S(2)}, u32[]{:S(2)}) %collective-permute-start.16) | collective-permute-done | bytes 32800 | tf_op jit(solution)/shard_map/ppermute | solution.py:275
  43.4 0.6 %collective-permute-done.15.r1 = bf16[128,128]{1,0:T(8,128)(2,1)S(1)} collective-permute-done((bf16[128,128]{1,0:T(8,128)(2,1)S(1)}, bf16[128,128]{1,0:T(8,128)(2,1)S(1)}, u32[]{:S(2)}, u32[]{:S(2)}) %collective-permute-start.15) | collective-permute-done | bytes 32800 | tf_op jit(solution)/shard_map/ppermute | solution.py:275
  44.1 0.4 collective-permute-start.20
  44.4 0.7 %shard_map.92 = (f32[256,128]{1,0:T(8,128)S(1)}, bf16[256,128]{1,0:T(8,128)(2,1)S(1)}, bf16[256,128]{1,0:T(8,128)(2,1)S(1)}, bf16[256,128]{1,0:T(8,128)(2,1)S(1)}) custom-call(s32[5]{0:T(128)S(1)} %stack.23.pos, f32[1024,128]{1,0:T(8,128)S(1)} %shard_map.90.keep, bf16[1024,128]{1,0:T(8,128)(2,1)S(1)} %collective-permute-done.9.r1, ...), custom_call_target="tpu_custom_call" | custom-call | tf_op jit(solution)/shard_map/pallas_call | solution.py:278
  45.2 4.9 %collective-permute-start.13 = (bf16[256,128]{1,0:T(8,128)(2,1)S(1)}, bf16[256,128]{1,0:T(8,128)(2,1)S(1)}, u32[]{:S(2)}, u32[]{:S(2)}) collective-permute-start(bf16[256,128]{1,0:T(8,128)(2,1)S(1)} %get-tuple-element.23), channel_id=1, source_target_pairs={{0,128},{64,192},{128,0},{192,64},{1,129},{65,193},{129,1},{193,65... | collective-permute-start | bytes 196616 | tf_op jit(solution)/shard_map/ppermute | solution.py:275
  50.2 2.9 %collective-permute-start.14 = (bf16[256,128]{1,0:T(8,128)(2,1)S(1)}, bf16[256,128]{1,0:T(8,128)(2,1)S(1)}, u32[]{:S(2)}, u32[]{:S(2)}) collective-permute-start(bf16[256,128]{1,0:T(8,128)(2,1)S(1)} %get-tuple-element.24), channel_id=1, source_target_pairs={{0,192},{64,0},{128,64},{192,128},{1,193},{65,1},{129,65},{193,129... | collective-permute-start | bytes 196616 | tf_op jit(solution)/shard_map/ppermute | solution.py:275
  53.1 2.1 %collective-permute-start.19 = (bf16[128,128]{1,0:T(8,128)(2,1)S(1)}, bf16[128,128]{1,0:T(8,128)(2,1)S(1)}, u32[]{:S(2)}, u32[]{:S(2)}) collective-permute-start(bf16[128,128]{1,0:T(8,128)(2,1)S(1)} %shard_map.93.w0), channel_id=1, source_target_pairs={{0,32},{16,48},{32,0},{48,16},{1,33},{17,49},{33,1},{49,17},{2,34}... | collective-permute-start | bytes 98312 | tf_op jit(solution)/shard_map/ppermute | solution.py:275
  55.2 3.3 %collective-permute-done.19.w2 = bf16[128,128]{1,0:T(8,128)(2,1)S(1)} collective-permute-done((bf16[128,128]{1,0:T(8,128)(2,1)S(1)}, bf16[128,128]{1,0:T(8,128)(2,1)S(1)}, u32[]{:S(2)}, u32[]{:S(2)}) %collective-permute-start.19) | collective-permute-done | bytes 32800 | tf_op jit(solution)/shard_map/ppermute | solution.py:275
  58.5 1.8 %collective-permute-done.18.w1 = bf16[128,128]{1,0:T(8,128)(2,1)S(1)} collective-permute-done((bf16[128,128]{1,0:T(8,128)(2,1)S(1)}, bf16[128,128]{1,0:T(8,128)(2,1)S(1)}, u32[]{:S(2)}, u32[]{:S(2)}) %collective-permute-start.18) | collective-permute-done | bytes 32800 | tf_op jit(solution)/shard_map/ppermute | solution.py:275
  60.3 0.7 %shard_map.94 = (bf16[256,128]{1,0:T(8,128)(2,1)}, f32[128,128]{1,0:T(8,128)}) custom-call(f32[256,128]{1,0:T(8,128)S(1)} %get-tuple-element.21.keep_z, bf16[256,128]{1,0:T(8,128)(2,1)S(1)} %collective-permute-done.12.r1, bf16[256,128]{1,0:T(8,128)(2,1)S(1)} %collective-permute-done.13.r2, bf16[256,128]{1,0:T(8,128)(2,1)S(1)} %collective-permute-done.14.r3, ...), custom_call_target="tpu_custom_call" | custom-call | tf_op jit(solution)/shard_map/pallas_call | solution.py:290
  (21 shorter events, 1.3 us)
Async XLA Ops:
  1.8 1.4 %collective-permute-start = (bf16[256,256]{1,0:T(8,128)(2,1)S(1)}, bf16[256,256]{1,0:T(8,128)(2,1)S(1)}, u32[]{:S(2)}, u32[]{:S(2)}) collective-permute-start(bf16[256,256]{1,0:T(8,128)(2,1)S(1)} %shard_map.87.own), channel_id=1, source_target_pairs={{0,1},{1,0},{2,3},{3,2},{4,5},{5,4},{6,7},{7,6},{8,9},{9,8},{10,11... | collective-permute-start | bytes 393224 | tf_op jit(solution)/shard_map/ppermute | solution.py:228
  3.8 10.9 %collective-permute-start.4 = (bf16[320,256]{1,0:T(8,128)(2,1)S(1)}, bf16[320,256]{1,0:T(8,128)(2,1)S(1)}, u32[]{:S(2)}, u32[]{:S(2)}) collective-permute-start(bf16[320,256]{1,0:T(8,128)(2,1)S(1)} %shard_map.88.refs_0_), channel_id=1, source_target_pairs={{0,6},{1,15},{2,0},{3,9},{4,2},{5,11},{6,4},{7,13},{8,14},{9,7},{1... | collective-permute-start | bytes 491528 | tf_op jit(solution)/shard_map/ppermute | solution.py:243
  6.6 9.8 %collective-permute-start.3 = (bf16[320,256]{1,0:T(8,128)(2,1)S(1)}, bf16[320,256]{1,0:T(8,128)(2,1)S(1)}, u32[]{:S(2)}, u32[]{:S(2)}) collective-permute-start(bf16[320,256]{1,0:T(8,128)(2,1)S(1)} %shard_map.88.refs_0_), channel_id=1, source_target_pairs={{0,4},{1,13},{2,6},{3,15},{4,0},{5,9},{6,2},{7,11},{8,12},{9,5},{1... | collective-permute-start | bytes 491528 | tf_op jit(solution)/shard_map/ppermute | solution.py:243
  7.4 10.6 %collective-permute-start.2 = (bf16[320,256]{1,0:T(8,128)(2,1)S(1)}, bf16[320,256]{1,0:T(8,128)(2,1)S(1)}, u32[]{:S(2)}, u32[]{:S(2)}) collective-permute-start(bf16[320,256]{1,0:T(8,128)(2,1)S(1)} %shard_map.88.refs_0_), channel_id=1, source_target_pairs={{0,2},{1,11},{2,4},{3,13},{4,6},{5,15},{6,0},{7,9},{8,10},{9,3},{1... | collective-permute-start | bytes 491528 | tf_op jit(solution)/shard_map/ppermute | solution.py:243
  8.3 9.8 %collective-permute-start.1 = (bf16[320,256]{1,0:T(8,128)(2,1)S(1)}, bf16[320,256]{1,0:T(8,128)(2,1)S(1)}, u32[]{:S(2)}, u32[]{:S(2)}) collective-permute-start(bf16[320,256]{1,0:T(8,128)(2,1)S(1)} %shard_map.88.refs_0_), channel_id=1, source_target_pairs={{1,9},{3,11},{5,13},{7,15},{9,1},{11,3},{13,5},{15,7},{17,25},{19,... | collective-permute-start | bytes 491528 | tf_op jit(solution)/shard_map/ppermute | solution.py:243
  16.4 2.2 %collective-permute-start.7 = (bf16[320,256]{1,0:T(8,128)(2,1)S(1)}, bf16[320,256]{1,0:T(8,128)(2,1)S(1)}, u32[]{:S(2)}, u32[]{:S(2)}) collective-permute-start(bf16[320,256]{1,0:T(8,128)(2,1)S(1)} %collective-permute-done.3.refs_3_), channel_id=1, source_target_pairs={{0,1},{1,0},{2,3},{3,2},{4,5},{5,4},{6,7},{7,6},{8,9},{9,8},{10,11... | collective-permute-start | bytes 491528 | tf_op jit(solution)/shard_map/ppermute | solution.py:249
  18.1 1.4 %collective-permute-start.6 = (bf16[320,256]{1,0:T(8,128)(2,1)S(1)}, bf16[320,256]{1,0:T(8,128)(2,1)S(1)}, u32[]{:S(2)}, u32[]{:S(2)}) collective-permute-start(bf16[320,256]{1,0:T(8,128)(2,1)S(1)} %collective-permute-done.2.refs_2_), channel_id=1, source_target_pairs={{0,1},{1,0},{2,3},{3,2},{4,5},{5,4},{6,7},{7,6},{8,9},{9,8},{10,11... | collective-permute-start | bytes 491528 | tf_op jit(solution)/shard_map/ppermute | solution.py:249
  18.1 1.6 %collective-permute-start.5 = (bf16[320,256]{1,0:T(8,128)(2,1)S(1)}, bf16[320,256]{1,0:T(8,128)(2,1)S(1)}, u32[]{:S(2)}, u32[]{:S(2)}) collective-permute-start(bf16[320,256]{1,0:T(8,128)(2,1)S(1)} %collective-permute-done.1.refs_1_), channel_id=1, source_target_pairs={{0,1},{1,0},{2,3},{3,2},{4,5},{5,4},{6,7},{7,6},{8,9},{9,8},{10,11... | collective-permute-start | bytes 491528 | tf_op jit(solution)/shard_map/ppermute | solution.py:249
  18.6 1.4 %collective-permute-start.8 = (bf16[320,256]{1,0:T(8,128)(2,1)S(1)}, bf16[320,256]{1,0:T(8,128)(2,1)S(1)}, u32[]{:S(2)}, u32[]{:S(2)}) collective-permute-start(bf16[320,256]{1,0:T(8,128)(2,1)S(1)} %collective-permute-done.4.refs_4_), channel_id=1, source_target_pairs={{0,1},{1,0},{2,3},{3,2},{4,5},{5,4},{6,7},{7,6},{8,9},{9,8},{10,11... | collective-permute-start | bytes 491528 | tf_op jit(solution)/shard_map/ppermute | solution.py:249
  21.3 23.1 %collective-permute-start.10 = (bf16[1024,128]{1,0:T(8,128)(2,1)S(1)}, bf16[1024,128]{1,0:T(8,128)(2,1)S(1)}, u32[]{:S(2)}, u32[]{:S(2)}) collective-permute-start(bf16[1024,128]{1,0:T(8,128)(2,1)S(1)} %get-tuple-element.19), channel_id=1, source_target_pairs={{0,32},{16,48},{32,0},{48,16},{1,33},{17,49},{33,1},{49,17},{2,34}... | collective-permute-start | bytes 786440 | tf_op jit(solution)/shard_map/ppermute | solution.py:275
  26.2 18.2 %collective-permute-start.9 = (bf16[1024,128]{1,0:T(8,128)(2,1)S(1)}, bf16[1024,128]{1,0:T(8,128)(2,1)S(1)}, u32[]{:S(2)}, u32[]{:S(2)}) collective-permute-start(bf16[1024,128]{1,0:T(8,128)(2,1)S(1)} %get-tuple-element.18), channel_id=1, source_target_pairs={{0,16},{16,32},{32,48},{48,0},{1,17},{17,33},{33,49},{49,1},{2,18}... | collective-permute-start | bytes 786440 | tf_op jit(solution)/shard_map/ppermute | solution.py:275
  26.5 18.0 %collective-permute-start.11 = (bf16[1024,128]{1,0:T(8,128)(2,1)S(1)}, bf16[1024,128]{1,0:T(8,128)(2,1)S(1)}, u32[]{:S(2)}, u32[]{:S(2)}) collective-permute-start(bf16[1024,128]{1,0:T(8,128)(2,1)S(1)} %get-tuple-element.20), channel_id=1, source_target_pairs={{0,48},{16,0},{32,16},{48,32},{1,49},{17,1},{33,17},{49,33},{2,50}... | collective-permute-start | bytes 786440 | tf_op jit(solution)/shard_map/ppermute | solution.py:275
  29.5 7.7 %collective-permute-start.17 = (bf16[128,128]{1,0:T(8,128)(2,1)S(1)}, bf16[128,128]{1,0:T(8,128)(2,1)S(1)}, u32[]{:S(2)}, u32[]{:S(2)}) collective-permute-start(bf16[128,128]{1,0:T(8,128)(2,1)S(1)} %get-tuple-element.25.own), channel_id=1, source_target_pairs={{0,192},{64,0},{128,64},{192,128},{1,193},{65,1},{129,65},{193,129... | collective-permute-start | bytes 98312 | tf_op jit(solution)/shard_map/ppermute | solution.py:275
  35.6 7.8 %collective-permute-start.16 = (bf16[128,128]{1,0:T(8,128)(2,1)S(1)}, bf16[128,128]{1,0:T(8,128)(2,1)S(1)}, u32[]{:S(2)}, u32[]{:S(2)}) collective-permute-start(bf16[128,128]{1,0:T(8,128)(2,1)S(1)} %get-tuple-element.25.own), channel_id=1, source_target_pairs={{0,128},{64,192},{128,0},{192,64},{1,129},{65,193},{129,1},{193,65... | collective-permute-start | bytes 98312 | tf_op jit(solution)/shard_map/ppermute | solution.py:275
  37.2 6.9 %collective-permute-start.15 = (bf16[128,128]{1,0:T(8,128)(2,1)S(1)}, bf16[128,128]{1,0:T(8,128)(2,1)S(1)}, u32[]{:S(2)}, u32[]{:S(2)}) collective-permute-start(bf16[128,128]{1,0:T(8,128)(2,1)S(1)} %get-tuple-element.25.own), channel_id=1, source_target_pairs={{0,64},{64,128},{128,192},{192,0},{1,65},{65,129},{129,193},{193,1... | collective-permute-start | bytes 98312 | tf_op jit(solution)/shard_map/ppermute | solution.py:275
  44.1 11.1 %collective-permute-start.20 = (bf16[128,128]{1,0:T(8,128)(2,1)S(1)}, bf16[128,128]{1,0:T(8,128)(2,1)S(1)}, u32[]{:S(2)}, u32[]{:S(2)}) collective-permute-start(bf16[128,128]{1,0:T(8,128)(2,1)S(1)} %shard_map.93.w0), channel_id=1, source_target_pairs={{0,48},{16,0},{32,16},{48,32},{1,49},{17,1},{33,17},{49,33},{2,50}... | collective-permute-start | bytes 98312 | tf_op jit(solution)/shard_map/ppermute | solution.py:275
  45.1 15.2 %collective-permute-start.12 = (bf16[256,128]{1,0:T(8,128)(2,1)S(1)}, bf16[256,128]{1,0:T(8,128)(2,1)S(1)}, u32[]{:S(2)}, u32[]{:S(2)}) collective-permute-start(bf16[256,128]{1,0:T(8,128)(2,1)S(1)} %get-tuple-element.22), channel_id=1, source_target_pairs={{0,64},{64,128},{128,192},{192,0},{1,65},{65,129},{129,193},{193,1... | collective-permute-start | bytes 196616 | tf_op jit(solution)/shard_map/ppermute | solution.py:275
  45.2 15.1 %collective-permute-start.13 = (bf16[256,128]{1,0:T(8,128)(2,1)S(1)}, bf16[256,128]{1,0:T(8,128)(2,1)S(1)}, u32[]{:S(2)}, u32[]{:S(2)}) collective-permute-start(bf16[256,128]{1,0:T(8,128)(2,1)S(1)} %get-tuple-element.23), channel_id=1, source_target_pairs={{0,128},{64,192},{128,0},{192,64},{1,129},{65,193},{129,1},{193,65... | collective-permute-start | bytes 196616 | tf_op jit(solution)/shard_map/ppermute | solution.py:275
  50.2 10.2 %collective-permute-start.14 = (bf16[256,128]{1,0:T(8,128)(2,1)S(1)}, bf16[256,128]{1,0:T(8,128)(2,1)S(1)}, u32[]{:S(2)}, u32[]{:S(2)}) collective-permute-start(bf16[256,128]{1,0:T(8,128)(2,1)S(1)} %get-tuple-element.24), channel_id=1, source_target_pairs={{0,192},{64,0},{128,64},{192,128},{1,193},{65,1},{129,65},{193,129... | collective-permute-start | bytes 196616 | tf_op jit(solution)/shard_map/ppermute | solution.py:275
  53.1 5.4 %collective-permute-start.19 = (bf16[128,128]{1,0:T(8,128)(2,1)S(1)}, bf16[128,128]{1,0:T(8,128)(2,1)S(1)}, u32[]{:S(2)}, u32[]{:S(2)}) collective-permute-start(bf16[128,128]{1,0:T(8,128)(2,1)S(1)} %shard_map.93.w0), channel_id=1, source_target_pairs={{0,32},{16,48},{32,0},{48,16},{1,33},{17,49},{33,1},{49,17},{2,34}... | collective-permute-start | bytes 98312 | tf_op jit(solution)/shard_map/ppermute | solution.py:275
  55.2 5.1 %collective-permute-start.18 = (bf16[128,128]{1,0:T(8,128)(2,1)S(1)}, bf16[128,128]{1,0:T(8,128)(2,1)S(1)}, u32[]{:S(2)}, u32[]{:S(2)}) collective-permute-start(bf16[128,128]{1,0:T(8,128)(2,1)S(1)} %shard_map.93.w0), channel_id=1, source_target_pairs={{0,16},{16,32},{32,48},{48,0},{1,17},{17,33},{33,49},{49,1},{2,18}... | collective-permute-start | bytes 98312 | tf_op jit(solution)/shard_map/ppermute | solution.py:275
